TPU v7x, 128 devices: a whole 4x4x4 slice. The times are simulated.
128 devices in a mesh: inner: 16 (over z_lo, y, core), rows: 8 (over x, z_hi).
Axes of the slice: x: 4, y: 4, z: 4 (z_hi: 2, z_lo: 2; z = z_hi * 2 + z_lo), core: 2. Of those that a mesh axis runs over, the one named last changes fastest.
Arguments:
- left_u: bfloat16 [8, 64, 2048, 128], P('rows', 'inner'), may hold values from -6 to 6
- left_v: bfloat16 [8, 64, 2048, 128], P('rows', 'inner'), may hold values from -0.035888672 to 0.035888672
- tile_p: bfloat16 [8, 8, 2048, 128], P('rows'), may hold values from -6 to 6
- tile_q: bfloat16 [8, 8, 2048, 128], P('rows'), may hold values from -0.5390625 to 0.5390625
- sketch: bfloat16 [2048, 128], replicated, may hold values from -6 to 6
- tile_cols: int32 [8, 8], P('rows'), may hold values from 0 to 7
Outputs:
- new_left: float32 [8, 8, 2048, 128], P('rows', None, 'inner')
- new_right: float32 [8, 8, 2048, 128], P('rows', None, 'inner')
All inputs are finite; a program needn't handle non-finite values.
Results may differ from a plain program's by a relative error of at most 0.0023.
Values may be sent and summed in bfloat16 or wider, within the bound.
A program may use at most 128 MiB of HBM per device.

v0:
```python
import math

import jax
import jax.numpy as jnp
from jax import lax
from jax.sharding import PartitionSpec as P


def from_gram(gram, sample):
    order = gram.shape[0]
    ridge = 1e-06 * jnp.trace(gram) / order
    gram = gram + ridge * jnp.eye(order, dtype=jnp.float32)
    triangle = jnp.linalg.cholesky(gram)
    return jax.scipy.linalg.solve_triangular(triangle, sample.T, lower=True).T


def body(left_u, left_v, tile_p, tile_q, sketch, tile_cols):
    highest = lax.Precision.HIGHEST
    rows_here, per_row = tile_cols.shape
    width = sketch.shape[0]
    rank = sketch.shape[1]
    factor_scale = math.sqrt(width)
    count = rows_here * per_row
    gathered_u, gathered_v = (
        lax.all_gather(left_u, "rows", axis=0, tiled=True),
        lax.all_gather(left_v, "rows", axis=0, tiled=True),
    )
    targets = jnp.arange(count, dtype=jnp.int32)

    def partial_sample(target):
        row_id = target // per_row
        column = tile_cols[row_id, target % per_row]
        coupling = jnp.einsum(
            "kbr,kbs->krs", left_v[row_id], gathered_v[column], preferred_element_type=jnp.float32
        )
        sketched = jnp.einsum(
            "kbs,bt->kst", gathered_u[column], sketch, preferred_element_type=jnp.float32
        )
        coupled = jnp.einsum("krs,kst->krt", coupling, sketched, precision=highest).astype(
            jnp.bfloat16
        )
        return (
            jnp.einsum("kbr,krt->bt", left_u[row_id], coupled, preferred_element_type=jnp.float32),
            coupling,
        )

    samples, couplings = lax.map(partial_sample, targets)
    flat_p = tile_p.reshape(count, width, rank).astype(jnp.float32)
    flat_q = tile_q.reshape(count, width, rank)
    sketched_q = jnp.einsum("nbr,bt->nrt", flat_q, sketch, preferred_element_type=jnp.float32)
    row_block = width // lax.axis_size("inner")
    offset = lax.axis_index("inner") * row_block
    sample_sum = lax.psum(samples, "inner")
    tile_sample = jnp.einsum("nbr,nrt->nbt", flat_p, sketched_q, precision=highest)
    sample = tile_sample - sample_sum
    gram = jnp.einsum("nbr,nbs->nrs", sample, sample, precision=highest)
    ortho_basis = jax.vmap(from_gram)(gram, sample)
    basis_rows = lax.dynamic_slice_in_dim(ortho_basis, offset, row_block, 1)
    basis_half = ortho_basis.astype(jnp.bfloat16)

    def partial_right(target):
        row_id = target // per_row
        column = tile_cols[row_id, target % per_row]
        inner_a = jnp.einsum(
            "kbr,bt->krt", left_u[row_id], basis_half[target], preferred_element_type=jnp.float32
        )
        inner_b = jnp.einsum("krs,krt->kst", couplings[target], inner_a, precision=highest).astype(
            jnp.bfloat16
        )
        return jnp.einsum(
            "kbs,kst->bt", gathered_u[column], inner_b, preferred_element_type=jnp.float32
        )

    rights = lax.map(partial_right, targets)
    projected = lax.psum_scatter(rights, "inner", scatter_dimension=1, tiled=True)
    p_basis = jnp.einsum("nbr,nbt->nrt", flat_p, ortho_basis, precision=highest)
    q_rows = lax.dynamic_slice_in_dim(flat_q, offset, row_block, 1).astype(jnp.float32)
    new_right = jnp.einsum("nbr,nrt->nbt", q_rows, p_basis, precision=highest) - projected
    shape = (rows_here, per_row, row_block, rank)
    return ((basis_rows * factor_scale).reshape(shape), (new_right / factor_scale).reshape(shape))


def solution(mesh):
    return jax.shard_map(
        body,
        mesh=mesh,
        in_specs=(
            P("rows", "inner", None, None),
            P("rows", "inner", None, None),
            P("rows", None, None, None),
            P("rows", None, None, None),
            P(),
            P("rows", None),
        ),
        out_specs=(P("rows", None, "inner", None), P("rows", None, "inner", None)),
        check_vma=False,
    )
```

profile of v0, /device:TPU:1, one launch (start us, length us, event | category | flops | bytes accessed | tf_op | source)
XLA Modules:
  0.0 1023.5 jit_solution(10539677950583329390)
XLA Ops:
  8.7 190.4 %all-gather.5.cloned.1.call-done = bf16[8,4,2048,128]{3,2,1,0:T(8,128)(2,1)} async-done(((bf16[1,4,2048,128]{3,2,1,0:T(8,128)(2,1)}), bf16[8,4,2048,128]{3,2,1,0:T(8,128)(2,1)}) %all-gather.5.cloned.1.call-update) | async-done | bytes 16777232 | tf_op jit(solution)/shard_map/all_gather | solution.py:25
  199.2 186.1 %all-gather.3.cloned.1.call-done = bf16[8,4,2048,128]{3,2,1,0:T(8,128)(2,1)} async-done(((bf16[1,4,2048,128]{3,2,1,0:T(8,128)(2,1)}), bf16[8,4,2048,128]{3,2,1,0:T(8,128)(2,1)}) %all-gather.3.cloned.1.call-update) | async-done | bytes 16777232 | tf_op jit(solution)/shard_map/all_gather | solution.py:26
  385.3 108.3 %while.26 = (s32[]{:T(128)}, f32[8,2048,128]{1,2,0:T(8,128)}, f32[8,4,128,128]{2,3,1,0:T(8,128)}, s32[8]{0:T(128)S(1)}, s32[1,8]{1,0:T(1,128)S(1)}, /*index=5*/b...) while((s32[]{:T(128)}, f32[8,2048,128]{1,2,0:T(8,128)}, ...), condition=%wide.region_1.2_spmd, body=%wide.region_0.1_spmd.sunk | while | flops 906035200 | bytes 11535702 | solution.py:47
  390.3 3.7 bitcast_dynamic-update-slice_fusion.2
  394.1 2.3 fusion.77
  397.0 1.8 fusion.78
  403.9 3.7 bitcast_dynamic-update-slice_fusion.2
  407.6 2.3 fusion.77
  410.5 1.8 fusion.78
  417.5 3.7 bitcast_dynamic-update-slice_fusion.2
  421.1 2.3 fusion.77
  424.1 1.8 fusion.78
  431.0 3.7 bitcast_dynamic-update-slice_fusion.2
  434.7 2.3 fusion.77
  437.6 1.9 fusion.78
  444.6 3.7 bitcast_dynamic-update-slice_fusion.2
  448.2 2.3 fusion.77
  451.2 1.8 fusion.78
  458.1 3.7 bitcast_dynamic-update-slice_fusion.2
  461.8 2.3 fusion.77
  464.7 1.8 fusion.78
  471.6 3.7 bitcast_dynamic-update-slice_fusion.2
  475.3 2.3 fusion.77
  478.2 1.8 fusion.78
  485.1 3.7 bitcast_dynamic-update-slice_fusion.2
  488.8 2.3 fusion.77
  491.8 1.8 fusion.78
  493.9 3.0 fusion.30
  496.9 136.6 %all-reduce.2.cloned.1.call-done = f32[8,2048,128]{1,2,0:T(8,128)} async-done(((f32[8,2048,128]{1,2,0:T(8,128)}), f32[8,2048,128]{1,2,0:T(8,128)}) %all-reduce.2.cloned.1.call-update) | async-done | bytes 8388624 | tf_op jit(solution)/shard_map/psum | solution.py:53
  633.5 8.1 bitcast_subtract_fusion
  641.6 8.0 select_reduce_fusion.1
  650.8 94.6 %custom-call.8 = f32[8,128,128]{2,1,0:T(8,128)S(1)} custom-call(f32[8,128,128]{2,1,0:T(8,128)} %fusion.37), custom_call_target="Cholesky" | custom-call | tf_op jit(solution)/shard_map/vmap(jit(cholesky))/cholesky | solution.py:13
  745.7 78.6 %custom-call.9 = f32[8,1,128,128]{2,3,1,0:T(8,128)S(1)} custom-call(f32[8,1,128,128]{3,2,1,0:T(8,128)S(1)} %select_bitcast_fusion), custom_call_target="InvertDiagBlocksLowerTriangular" | custom-call | tf_op jit(solution)/shard_map/vmap(jit(_solve_triangular))/triangular_solve | solution.py:14
  824.3 10.2 fusion.34
  834.5 3.1 convert_bitcast_fusion
  837.6 1.5 copy-done.2
  839.1 102.1 %while.27 = (s32[]{:T(128)}, f32[8,2048,128]{2,1,0:T(8,128)}, s32[8]{0:T(128)S(1)}, s32[1,8]{1,0:T(1,128)S(1)}, bf16[8,4,2048,128]{3,2,1,0:T(8,128)(2,1)}, /*ind...) while((s32[]{:T(128)}, f32[8,2048,128]{2,1,0:T(8,128)}, ...), condition=%wide.region_7.8_spmd, body=%wide.region_6.7_spmd.sunk | while | flops 637599744 | bytes 6816611 | solution.py:74
  845.5 1.5 fusion.85
  847.0 1.6 convolution_convert_fusion.5
  848.6 3.3 fusion.86
  858.3 1.5 fusion.85
  859.8 1.6 convolution_convert_fusion.5
  861.4 3.3 fusion.86
  871.0 1.5 fusion.85
  872.5 1.6 convolution_convert_fusion.5
  874.1 3.3 fusion.86
  883.8 1.5 fusion.85
  885.3 1.6 convolution_convert_fusion.5
  886.9 3.3 fusion.86
  896.5 1.5 fusion.85
  898.0 1.6 convolution_convert_fusion.5
  899.7 3.3 fusion.86
  909.4 1.5 fusion.85
  910.8 1.6 convolution_convert_fusion.5
  912.5 3.3 fusion.86
  922.1 1.5 fusion.85
  923.6 1.6 convolution_convert_fusion.5
  925.2 3.3 fusion.86
  934.9 1.5 fusion.85
  936.4 1.6 convolution_convert_fusion.5
  938.0 3.3 fusion.86
  943.4 8.7 fusion.27
  952.1 62.3 %reduce-scatter.2.cloned.1.call-done = f32[8,128,128]{2,1,0:T(8,128)} async-done(((f32[8,2048,128]{2,1,0:T(8,128)}), f32[8,128,128]{2,1,0:T(8,128)}) %reduce-scatter.2.cloned.1.call-update) | async-done | bytes 524304 | tf_op jit(solution)/shard_map/reduce_scatter | solution.py:75
  1014.4 2.6 fusion.33
  (73 shorter events, 29.4 us)
Async XLA Ops:
  7.2 378.1 %copy-start = (bf16[1,4,2048,128]{3,2,1,0:T(8,128)(2,1)S(1)}, bf16[1,4,2048,128]{3,2,1,0:T(8,128)(2,1)}, u32[]{:S(2)}) copy-start(bf16[1,4,2048,128]{3,2,1,0:T(8,128)(2,1)} %param.10) | copy-start | bytes 6291460
  7.2 378.1 %copy-start.3 = (bf16[2048,128]{1,0:T(8,128)(2,1)S(1)}, bf16[2048,128]{1,0:T(8,128)(2,1)}, u32[]{:S(2)}) copy-start(bf16[2048,128]{1,0:T(8,128)(2,1)} %param.14) | copy-start | bytes 1572868
  7.2 378.1 %copy-start.4 = (s32[1,8]{1,0:T(1,128)S(1)}, s32[1,8]{1,0:T(1,128)}, u32[]{:S(2)}) copy-start(s32[1,8]{1,0:T(1,128)} %param.15) | copy-start | bytes 100
  7.2 192.0 %all-gather.5.cloned.1.call-start = ((), (), s32[]{:S(2)}) async-start(), calls=%async_computation.2 | async-start | bytes 18874368 | tf_op jit(solution)/shard_map/all_gather | solution.py:25
  7.9 377.3 %all-gather.3.cloned.1.call-start = ((), (), s32[]{:S(2)}) async-start(), calls=%async_computation.1 | async-start | bytes 18874368 | tf_op jit(solution)/shard_map/all_gather | solution.py:26
  8.7 624.8 %all-reduce.2.cloned.1.call-start = ((), (), s32[]{:S(2)}) async-start(), calls=%async_computation.3 | async-start | bytes 16777216 | tf_op jit(solution)/shard_map/psum | solution.py:53
  493.6 520.8 %reduce-scatter.2.cloned.1.call-start = ((), (), s32[]{:S(2)}) async-start(), calls=%async_computation.4 | async-start | bytes 8912896 | tf_op jit(solution)/shard_map/reduce_scatter | solution.py:75
  641.6 8.1 copy-start.1
  834.5 4.6 copy-start.2
Sparse Core Ops, SparseCore 0:
  10.4 188.7 all-gather.4
  201.5 183.6 all-gather.2
  493.7 139.6 all-reduce.1
  941.4 72.9 reduce-scatter.1
where the time goes:
time: 1030 us; the launch traced here: 1020 us
  waiting for transfers between devices  577 us (56%)
  other arithmetic  179 us (17%)
  matrix products  159 us (15%)
  loops' own time  72.5 us (7%)
  local copies, waits for them, and re-layouts  21.9 us (2%)
  between operations  13.9 us (1%)
    all_gather x1, waiting for transfers between devices, body(): lax.all_gather(left_u, 'rows', axis=0, tiled=True)  190 us
    all_gather x1, waiting for transfers between devices, body(): lax.all_gather(left_v, 'rows', axis=0, tiled=True)  186 us
    psum x1, waiting for transfers between devices, body(): sample_sum = lax.psum(samples, 'inner')  137 us
    another operation x4, other arithmetic, from_gram(): triangle = jnp.linalg.cholesky(gram)  94.7 us
    another operation x3, other arithmetic, from_gram(): return jax.scipy.linalg.solve_triangular(triangle, sample.T, lower=True).T  78.7 us
    reduce_scatter x1, waiting for transfers between devices, body(): lax.psum_scatter(rights, 'inner', scatter_dimension=1, tiled=True)  62.3 us
    another operation x1, loops' own time, body(): rights = lax.map(partial_right, targets)  41.1 us
    another operation x1, loops' own time, body(): samples, couplings = lax.map(partial_sample, targets)  31.3 us
  transfers between devices with their start and end apart: 4, of which 4 were waited for; matrix products, arithmetic and copies ran while one was open for 1% of the time, Pallas kernels for 0%

commit v1 on v0

v1 whole, which is shorter than its diff:
```python
import math

import jax
import jax.numpy as jnp
from jax import lax
from jax.experimental import pallas as pl
from jax.experimental.pallas import tpu as pltpu
from jax.sharding import PartitionSpec as P

MESH = pl.DeviceIdType.MESH
HIGHEST = lax.Precision.HIGHEST
F32 = jnp.float32
BF16 = jnp.bfloat16
VMEM_LIMIT = 56 * 1024 * 1024


def device(row, place):
    return {"rows": row, "inner": place}


def greet(partners, count):
    barrier = pltpu.get_barrier_semaphore()
    for row, place in partners:
        pl.semaphore_signal(barrier, inc=1, device_id=device(row, place), device_id_type=MESH)
    pl.semaphore_wait(barrier, count)


def remote(src, dst, send_sem, recv_sem, row, place):
    return pltpu.make_async_remote_copy(
        src_ref=src, dst_ref=dst, send_sem=send_sem, recv_sem=recv_sem,
        device_id=device(row, place), device_id_type=MESH,
    )


class Send:
    def __init__(self, src, dst, send_sem, recv_sem, row, place, is_self):
        self.far = remote(src, dst, send_sem, recv_sem, row, place)
        self.near = pltpu.make_async_copy(src, dst, recv_sem)
        self.is_self = is_self

    def start(self):
        @pl.when(jnp.logical_not(self.is_self))
        def _():
            self.far.start()

        @pl.when(self.is_self)
        def _():
            self.near.start()

    def wait_send(self):
        @pl.when(jnp.logical_not(self.is_self))
        def _():
            self.far.wait_send()


def arrived(ref, sem):
    pltpu.make_async_copy(ref, ref, sem).wait()


def dot(a, b, precision=None):
    return jnp.dot(a, b, preferred_element_type=F32, precision=precision)


def dot_t(a, b, precision=None):
    return lax.dot_general(
        a, b, (((0,), (0,)), ((), ())), preferred_element_type=F32, precision=precision
    )


def dot_nt(a, b, precision=None):
    return lax.dot_general(
        a, b, (((1,), (1,)), ((), ())), preferred_element_type=F32, precision=precision
    )


def couple_kernel(
    v_ref, u_ref, sketch_ref, coupled_ref, coupling_ref,
    vbuf, sown, sbuf, gown, gout, gsib, cown,
    v_send, v_recv, s_send, s_recv, g_send, g_recv, c_send, c_recv, k_send, k_recv,
):
    row, me = lax.axis_index("rows"), lax.axis_index("inner")
    core = lax.rem(me, 2)
    base = me - core
    sib = base + 1 - core
    owner_core = row // 4
    slot = lax.rem(row, 4)

    partners = [(lax.rem(row + d, 8), base + h) for d in range(1, 8) for h in range(2)]
    greet(partners + [(row, sib)], 15)

    v_copies = []
    for kk in range(4):
        for hh in range(2):
            to = core * 4 + kk
            v_copies.append(
                Send(
                    v_ref.at[kk, pl.ds(hh * 1024, 1024), :],
                    vbuf.at[:, pl.ds(pl.multiple_of(row * 128, 128), 128)],
                    v_send.at[kk * 2 + hh], v_recv.at[row], to, base + hh,
                    jnp.logical_and(to == row, core == hh),
                )
            )
            v_copies[-1].start()

    s_copies = []
    for kk in range(4):
        sown[kk] = dot_t(u_ref[kk], sketch_ref[...])
        to = core * 4 + kk
        s_copies.append(
            Send(
                sown.at[kk], sbuf.at[slot], s_send.at[kk], s_recv.at[slot],
                to, base + owner_core, jnp.logical_and(to == row, core == owner_core),
            )
        )
        s_copies[-1].start()

    for i in range(8):
        arrived(vbuf.at[:, pl.ds(i * 128, 128)], v_recv.at[i])

    def gram_half(half, out):
        right = vbuf[:, pl.ds(pl.multiple_of(half * 512, 512), 512)]
        for pair in range(4):
            value = dot_t(vbuf[:, pl.ds(pair * 256, 256)], right)
            for p in range(2):
                for j in range(4):
                    out[pair * 2 + p, j] = value[p * 128 : p * 128 + 128, j * 128 : j * 128 + 128]

    gram_half(1 - core, gout)
    g_copy = remote(gout, gsib, g_send, g_recv, row, sib)
    g_copy.start()
    gram_half(core, gown)
    g_copy.wait_recv()

    for j in range(4):
        arrived(sbuf.at[j], s_recv.at[j])
    for i in range(8):
        for j in range(4):
            total = gown[i, j] + gsib[i, j]
            gown[i, j] = total
            cown[i * 128 : i * 128 + 128, j * 128 : j * 128 + 128] = dot(
                total, sbuf[j], HIGHEST
            ).astype(BF16)

    c_copies = []
    for i in range(8):
        is_self = jnp.logical_and(row == i, core == owner_core)
        c_copies.append(
            Send(
                cown.at[pl.ds(i * 128, 128), :],
                coupled_ref.at[
                    pl.ds(pl.multiple_of(slot * 128, 128), 128),
                    pl.ds(pl.multiple_of(core * 512, 512), 512),
                ],
                c_send.at[i], c_recv.at[slot * 2 + core], i, base + owner_core, is_self,
            )
        )
        c_copies[-1].start()
    for i in range(8):
        is_self = jnp.logical_and(row == i, core == owner_core)
        c_copies.append(
            Send(
                gown.at[i], coupling_ref.at[slot, pl.ds(core * 4, 4)],
                k_send.at[i], k_recv.at[slot * 2 + core], i, base + owner_core, is_self,
            )
        )
        c_copies[-1].start()
    for kk in range(4):
        for hh in range(2):
            arrived(
                coupled_ref.at[pl.ds(kk * 128, 128), pl.ds(hh * 512, 512)],
                c_recv.at[kk * 2 + hh],
            )
            arrived(coupling_ref.at[kk, pl.ds(hh * 4, 4)], k_recv.at[kk * 2 + hh])
    for copy in v_copies + s_copies + [g_copy] + c_copies:
        copy.wait_send()


def couple(v, u, sketch):
    dma = pltpu.SemaphoreType.DMA
    vmem = pl.BlockSpec(memory_space=pltpu.VMEM)
    hbm = pl.BlockSpec(memory_space=pl.ANY)
    return pl.pallas_call(
        couple_kernel,
        out_shape=(
            jax.ShapeDtypeStruct((512, 1024), BF16),
            jax.ShapeDtypeStruct((4, 8, 128, 128), F32),
        ),
        in_specs=[hbm, vmem, vmem],
        out_specs=(hbm, hbm),
        scratch_shapes=[
            pltpu.VMEM((1024, 1024), BF16),
            pltpu.VMEM((4, 128, 128), F32),
            pltpu.VMEM((4, 128, 128), F32),
            pltpu.VMEM((8, 4, 128, 128), F32),
            pltpu.VMEM((8, 4, 128, 128), F32),
            pltpu.VMEM((8, 4, 128, 128), F32),
            pltpu.VMEM((1024, 512), BF16),
            dma((8,)), dma((8,)), dma((4,)), dma((4,)), dma, dma,
            dma((8,)), dma((8,)), dma((8,)), dma((8,)),
        ],
        compiler_params=pltpu.CompilerParams(
            collective_id=1, has_side_effects=True, vmem_limit_bytes=VMEM_LIMIT
        ),
        cost_estimate=pl.CostEstimate(
            flops=2_500_000_000, bytes_accessed=60_000_000, transcendentals=0
        ),
    )(v, u, sketch)


def neighbours(row, me):
    return [(row, lax.rem(me + d, 16)) for d in range(1, 16)]


def chip_at(chip, step):
    z, y = chip // 4, lax.rem(chip, 4)
    return lax.rem(z + step[0], 2) * 4 + lax.rem(y + step[1], 4)


def chip_back(chip, step):
    z, y = chip // 4, lax.rem(chip, 4)
    return lax.rem(z + step[0], 2) * 4 + lax.rem(y + 4 - step[1], 4)


STEPS = [(1, 2), (0, 2), (1, 1), (1, 3), (0, 1), (0, 3), (1, 0)]


def sample_kernel(
    cols_ref, u_ref, coupled_ref, p_ref, sq_ref, sample_ref, gram_ref,
    dpart, tosib, sibbuf, rsbuf, dsum, gpart, grbuf,
    i_send, i_recv, x_send, x_recv, gr_send, gr_recv,
):
    row, me = lax.axis_index("rows"), lax.axis_index("inner")
    core = lax.rem(me, 2)
    chip = me // 2
    sib = chip * 2 + 1 - core
    greet(neighbours(row, me), 15)

    steps = STEPS + [(0, 0)]
    inner_copies, chip_copies = [], []

    def pass_on(n):
        inner_copies[n].wait_recv()
        dpart[n] = dpart[n] + sibbuf[n]
        if n < 7:
            target = chip_at(chip, steps[n])
            copy = remote(
                dpart.at[n], rsbuf.at[n], x_send.at[n], x_recv.at[n], row, target * 2 + core
            )
            copy.start()
            chip_copies.append(copy)

    for n, step in enumerate(steps):
        target = chip_at(chip, step)
        for h in range(2):
            which = core if h else 1 - core
            rows = pl.ds(pl.multiple_of(target * 256 + which * 128, 128), 128)
            left = jnp.concatenate([u_ref[kk, rows, :] for kk in range(4)], axis=1)
            part = dot(left, coupled_ref[...])
            if h:
                dpart[n] = part
            else:
                tosib[n] = part
                copy = remote(tosib.at[n], sibbuf.at[n], i_send.at[n], i_recv.at[n], row, sib)
                copy.start()
                inner_copies.append(copy)
        if n >= 1:
            pass_on(n - 1)
    pass_on(7)
    total = dpart[7]
    for n in range(7):
        chip_copies[n].wait_recv()
        total = total + rsbuf[n]
    for j in range(8):
        dsum[j] = total[:, j * 128 : j * 128 + 128]

    gram_copies = []
    for c in range(8):
        value = dot(p_ref[c].astype(F32), sq_ref[c], HIGHEST) - dsum[cols_ref[c]]
        sample_ref[c] = value
        gpart[c] = dot_t(value, value, HIGHEST)
        for h in range(2):
            copy = Send(
                gpart.at[c], grbuf.at[me], gr_send.at[c * 2 + h], gr_recv.at[me],
                row, c * 2 + h, me == c * 2 + h,
            )
            copy.start()
            gram_copies.append(copy)
    gram = jnp.zeros((128, 128), F32)
    for m in range(16):
        arrived(grbuf.at[m], gr_recv.at[m])
        gram = gram + grbuf[m]
    gram_ref[...] = gram
    for copy in inner_copies + chip_copies + gram_copies:
        copy.wait_send()


def make_sample(cols, u, coupled, p_rows, sketched_q):
    dma = pltpu.SemaphoreType.DMA
    vmem = pl.BlockSpec(memory_space=pltpu.VMEM)
    smem = pl.BlockSpec(memory_space=pltpu.SMEM)
    return pl.pallas_call(
        sample_kernel,
        out_shape=(
            jax.ShapeDtypeStruct((8, 128, 128), F32),
            jax.ShapeDtypeStruct((128, 128), F32),
        ),
        in_specs=[smem, vmem, vmem, vmem, vmem],
        out_specs=(vmem, vmem),
        scratch_shapes=[
            pltpu.VMEM((8, 128, 1024), F32),
            pltpu.VMEM((8, 128, 1024), F32),
            pltpu.VMEM((8, 128, 1024), F32),
            pltpu.VMEM((7, 128, 1024), F32),
            pltpu.VMEM((8, 128, 128), F32),
            pltpu.VMEM((8, 128, 128), F32),
            pltpu.VMEM((16, 128, 128), F32),
            dma((8,)), dma((8,)), dma((7,)), dma((7,)), dma((16,)), dma((16,)),
        ],
        compiler_params=pltpu.CompilerParams(
            collective_id=2, has_side_effects=True, vmem_limit_bytes=VMEM_LIMIT
        ),
        cost_estimate=pl.CostEstimate(
            flops=2_500_000_000, bytes_accessed=100_000_000, transcendentals=0
        ),
    )(cols, u, coupled, p_rows, sketched_q)


def basis_kernel(
    scale, linv_ref, sample_ref, left_ref, all_ref, lbuf, bown,
    l_send, l_recv, b_send, b_recv, f_send,
):
    row, me = lax.axis_index("rows"), lax.axis_index("inner")
    core = lax.rem(me, 2)
    chip = me // 2
    sib = chip * 2 + 1 - core
    greet(neighbours(row, me), 15)

    copies = []
    for n, step in enumerate(STEPS):
        target = chip_at(chip, step)
        copy = remote(
            linv_ref, lbuf.at[chip], l_send.at[n], l_recv.at[chip], row, target * 2 + core
        )
        copy.start()
        copies.append(copy)
    lbuf[chip] = linv_ref[...]
    for step in STEPS:
        source = chip_back(chip, step)
        arrived(lbuf.at[source], l_recv.at[source])
    for c in range(8):
        value = dot_nt(sample_ref[c], lbuf[c], HIGHEST)
        left_ref[c] = value * scale
        bown[:, c * 128 : c * 128 + 128] = value.astype(BF16)

    def block(m):
        return all_ref.at[pl.ds(pl.multiple_of(m * 128, 128), 128), :]

    for n, step in enumerate(STEPS):
        target = chip_at(chip, step)
        copy = remote(bown, block(me), b_send.at[n], b_recv.at[me], row, target * 2 + core)
        copy.start()
        copies.append(copy)
    copy = remote(bown, block(me), b_send.at[7], b_recv.at[me], row, sib)
    copy.start()
    copies.append(copy)
    all_ref[pl.ds(pl.multiple_of(me * 128, 128), 128), :] = bown[...]
    order = STEPS[::-1]
    for n, step in enumerate(order):
        m = chip_back(chip, step) * 2 + core
        arrived(block(m), b_recv.at[m])
        copy = remote(block(m), block(m), f_send.at[n], b_recv.at[m], row, sib)
        copy.start()
        copies.append(copy)
    arrived(block(sib), b_recv.at[sib])
    for step in order:
        m = chip_back(chip, step) * 2 + 1 - core
        arrived(block(m), b_recv.at[m])
    for copy in copies:
        copy.wait_send()


def make_basis(linv, sample, scale):
    dma = pltpu.SemaphoreType.DMA
    vmem = pl.BlockSpec(memory_space=pltpu.VMEM)

    def kernel(*refs):
        basis_kernel(scale, *refs)

    return pl.pallas_call(
        kernel,
        out_shape=(
            jax.ShapeDtypeStruct((8, 128, 128), F32),
            jax.ShapeDtypeStruct((2048, 1024), BF16),
        ),
        in_specs=[vmem, vmem],
        out_specs=(vmem, vmem),
        scratch_shapes=[
            pltpu.VMEM((8, 128, 128), F32),
            pltpu.VMEM((128, 1024), BF16),
            dma((7,)), dma((8,)), dma((8,)), dma((16,)), dma((7,)),
        ],
        compiler_params=pltpu.CompilerParams(
            collective_id=3, has_side_effects=True, vmem_limit_bytes=VMEM_LIMIT
        ),
        cost_estimate=pl.CostEstimate(
            flops=200_000_000, bytes_accessed=40_000_000, transcendentals=0
        ),
    )(linv, sample)


def right_kernel(
    scale, cols_ref, u_ref, basis_ref, coupling_ref, panel_ref, q_ref, pb_ref, right_ref,
    panel, ib, dpart, tosib, sibbuf, xbuf, rsbuf,
    p_sem, i_send, i_recv, x_send, x_recv,
):
    row, me = lax.axis_index("rows"), lax.axis_index("inner")
    core = lax.rem(me, 2)
    chip = me // 2
    sib = chip * 2 + 1 - core
    load = pltpu.make_async_copy(panel_ref, panel, p_sem)
    load.start()
    greet(neighbours(row, me), 15)

    for kk in range(4):
        ia = dot_t(u_ref[kk], basis_ref[...])
        for c in range(8):
            ib[kk * 128 : kk * 128 + 128, c * 128 : c * 128 + 128] = dot_t(
                coupling_ref[kk, cols_ref[c]], ia[:, c * 128 : c * 128 + 128], HIGHEST
            ).astype(BF16)
    load.wait()

    steps = STEPS + [(0, 0)]
    inner_copies, chip_copies = [], []

    def pass_on(n):
        inner_copies[n].wait_recv()
        if n < 7:
            target = chip_at(chip, steps[n])
            xbuf[n] = (dpart[n] + sibbuf[n]).astype(BF16)
            copy = remote(
                xbuf.at[n], rsbuf.at[n], x_send.at[n], x_recv.at[n], row, target * 2 + core
            )
            copy.start()
            chip_copies.append(copy)

    for n, step in enumerate(steps):
        target = chip_at(chip, step)
        for h in range(2):
            which = core if h else 1 - core
            rows = pl.ds(pl.multiple_of(target * 256 + which * 128, 128), 128)
            out = dpart if h else tosib
            for c in range(8):
                col = cols_ref[c]
                left = jnp.concatenate([panel[col, kk, rows, :] for kk in range(4)], axis=1)
                out[n, :, c * 128 : c * 128 + 128] = dot(left, ib[:, c * 128 : c * 128 + 128])
            if not h:
                copy = remote(tosib.at[n], sibbuf.at[n], i_send.at[n], i_recv.at[n], row, sib)
                copy.start()
                inner_copies.append(copy)
        if n >= 1:
            pass_on(n - 1)
    pass_on(7)
    total = dpart[7] + sibbuf[7]
    for n in range(7):
        chip_copies[n].wait_recv()
        total = total + rsbuf[n].astype(F32)
    for c in range(8):
        value = dot(q_ref[c].astype(F32), pb_ref[c], HIGHEST)
        right_ref[c] = (value - total[:, c * 128 : c * 128 + 128]) * (1.0 / scale)
    for copy in inner_copies + chip_copies:
        copy.wait_send()


def make_right(cols, u, basis, coupling, panel, q_rows, p_basis, scale):
    dma = pltpu.SemaphoreType.DMA
    vmem = pl.BlockSpec(memory_space=pltpu.VMEM)
    smem = pl.BlockSpec(memory_space=pltpu.SMEM)
    hbm = pl.BlockSpec(memory_space=pl.ANY)

    def kernel(*refs):
        right_kernel(scale, *refs)

    return pl.pallas_call(
        kernel,
        out_shape=jax.ShapeDtypeStruct((8, 128, 128), F32),
        in_specs=[smem, vmem, vmem, vmem, hbm, vmem, vmem],
        out_specs=vmem,
        scratch_shapes=[
            pltpu.VMEM((8, 4, 2048, 128), BF16),
            pltpu.VMEM((512, 1024), BF16),
            pltpu.VMEM((8, 128, 1024), F32),
            pltpu.VMEM((8, 128, 1024), F32),
            pltpu.VMEM((8, 128, 1024), F32),
            pltpu.VMEM((7, 128, 1024), BF16),
            pltpu.VMEM((7, 128, 1024), BF16),
            dma, dma((8,)), dma((8,)), dma((7,)), dma((7,)),
        ],
        compiler_params=pltpu.CompilerParams(
            collective_id=4, has_side_effects=True, vmem_limit_bytes=VMEM_LIMIT
        ),
        cost_estimate=pl.CostEstimate(
            flops=4_500_000_000, bytes_accessed=100_000_000, transcendentals=0
        ),
    )(cols, u, basis, coupling, panel, q_rows, p_basis)


def body(left_u, left_v, tile_p, tile_q, sketch, tile_cols):
    width, rank = sketch.shape
    factor_scale = math.sqrt(width)
    u, v, p, q, cols = left_u[0], left_v[0], tile_p[0], tile_q[0], tile_cols[0]
    row_block = width // lax.axis_size("inner")
    offset = lax.axis_index("inner") * row_block

    panel = lax.all_gather(u, "rows", axis=0)
    coupled, coupling = couple(v, u, sketch)
    sketched_q = jnp.einsum("nbr,bt->nrt", q, sketch, preferred_element_type=F32)
    p_rows = lax.dynamic_slice_in_dim(p, offset, row_block, 1)
    q_rows = lax.dynamic_slice_in_dim(q, offset, row_block, 1)
    sample, gram = make_sample(cols, u, coupled, p_rows, sketched_q)
    eye = jnp.eye(rank, dtype=F32)
    ridge = 1e-06 * jnp.trace(gram) / rank
    triangle = jnp.linalg.cholesky(gram + ridge * eye)
    inverse = jax.scipy.linalg.solve_triangular(triangle, eye, lower=True)
    new_left, basis = make_basis(inverse, sample, factor_scale)
    p_basis = jnp.einsum(
        "nbr,bnt->nrt", p, basis.reshape(width, -1, rank), preferred_element_type=F32
    )
    new_right = make_right(cols, u, basis, coupling, panel, q_rows, p_basis, factor_scale)
    return new_left[None], new_right[None]


def solution(mesh):
    return jax.shard_map(
        body,
        mesh=mesh,
        in_specs=(
            P("rows", "inner", None, None),
            P("rows", "inner", None, None),
            P("rows", None, None, None),
            P("rows", None, None, None),
            P(),
            P("rows", None),
        ),
        out_specs=(P("rows", None, "inner", None), P("rows", None, "inner", None)),
        check_vma=False,
    )
```

time: 1030 us -> 386 us (0.37)
  waiting for transfers between devices: 577 us -> 34.9 us
  Pallas kernels: 0 us -> 289 us
  other arithmetic: 179 us -> 26 us
  matrix products: 159 us -> 8.63 us
  loops' own time: 72.5 us -> 0 us
    all_gather x2 -> x1, waiting for transfers between devices: 377 us -> 34.2 us  [body(): panel = lax.all_gather(u, 'rows', axis=0)]
    pallas_call x0 -> x4, Pallas kernels: none -> 289 us  [the longest x1 105 us: couple(): pl.pallas_call(couple_kernel, out_shape=(jax.ShapeDtypeStruct((512, 1024)...]
    another operation x9 -> x5, other arithmetic: 173 us -> 22.9 us  [the longest x3 12.4 us: body(): triangle = jnp.linalg.cholesky(gram + ridge * eye)]
    dot_general x61 -> x2, matrix products: 149 us -> 7.74 us  [the longest x1 5.66 us: body(): jnp.einsum('nbr,bnt->nrt', p, basis.reshape(width, -1, rank), preferred_e...]
    psum x1 -> x0, waiting for transfers between devices: 137 us -> none  [body(): sample_sum = lax.psum(samples, 'inner')]
    another operation x2 -> x0, loops' own time: 72.5 us -> none  [the longest x1 41.1 us: body(): rights = lax.map(partial_right, targets)]
    reduce_scatter x1 -> x0, waiting for transfers between devices: 62.3 us -> none  [body(): lax.psum_scatter(rights, 'inner', scatter_dimension=1, tiled=True)]
    dynamic_slice x32 -> x2, local copies, waits for them, and re-layouts: 19.1 us -> 3.35 us  [the longest x1 1.68 us: body(): p_rows = lax.dynamic_slice_in_dim(p, offset, row_block, 1)]
  transfers between devices with their start and end apart: 4 -> 1, of which waited for: 4 -> 1; matrix products, arithmetic and copies ran while one was open for 1% -> 12% of each run, Pallas kernels for 0% -> 63%
where the time goes in v1:
time: 386 us
  Pallas kernels  289 us (75%)
  waiting for transfers between devices  34.9 us (9%)
  other arithmetic  26 us (7%)
  between operations  14.8 us (4%)
  local copies, waits for them, and re-layouts  12.6 us (3%)
  matrix products  8.63 us (2%)
    pallas_call x1, Pallas kernels, couple(): pl.pallas_call(couple_kernel, out_shape=(jax.ShapeDtypeStruct((512, 1024)...  105 us
    pallas_call x1, Pallas kernels, make_sample(): pl.pallas_call(sample_kernel, out_shape=(jax.ShapeDtypeStruct((8, 128, 12...  85.4 us
    pallas_call x1, Pallas kernels, make_basis(): pl.pallas_call(kernel, out_shape=(jax.ShapeDtypeStruct((8, 128, 128), F32...  53.5 us
    pallas_call x1, Pallas kernels, make_right(): pl.pallas_call(kernel, out_shape=jax.ShapeDtypeStruct((8, 128, 128), F32)...  45.2 us
    all_gather x1, waiting for transfers between devices, body(): panel = lax.all_gather(u, 'rows', axis=0)  34.2 us
    another operation x3, other arithmetic, body(): triangle = jnp.linalg.cholesky(gram + ridge * eye)  12.4 us
    another operation x2, other arithmetic, body(): inverse = jax.scipy.linalg.solve_triangular(triangle, eye, lower=True)  10.5 us
  transfers between devices with their start and end apart: 1, of which 1 were waited for; matrix products, arithmetic and copies ran while one was open for 12% of the time, Pallas kernels for 63%

profile of v1, /device:TPU:1, one launch (start us, length us, event | category | flops | bytes accessed | tf_op | source)
XLA Modules:
  0.0 385.8 jit_solution(13388941986987870725)
XLA Ops:
  7.2 0.0 all-gather.2.cloned.1.call-start
  7.2 0.7 all-gather.2.cloned.1.call-update
  7.9 1.7 dynamic-slice_bitcast_fusion.1.p_ref
  9.6 0.0 copy-start
  9.6 0.0 copy-start.1
  9.6 104.6 %shard_map.77 = (bf16[512,1024]{1,0:T(8,128)(2,1)}, f32[4,8,128,128]{3,2,1,0:T(8,128)}) custom-call(bf16[4,2048,128]{2,1,0:T(8,128)(2,1)} %bitcast.41, bf16[4,2048,128]{2,1,0:T(8,128)(2,1)} %bitcast.34, bf16[2048,128]{1,0:T(8,128)(2,1)} %sketch_ref.1), custom_call_target="tpu_custom_call" | custom-call | flops 2500000000 | bytes 60000000 | tf_op jit(solution)/shard_map/pallas_call | solution.py:182
  114.2 0.0 copy-done
  114.2 0.0 copy-done.1
  114.3 2.1 fusion.2.sq_ref
  116.3 85.4 %shard_map.78 = (f32[8,128,128]{2,1,0:T(8,128)}, f32[128,128]{1,0:T(8,128)}) custom-call(s32[8]{0:T(128)} %bitcast.39, bf16[4,2048,128]{2,1,0:T(8,128)(2,1)} %bitcast.35, bf16[512,1024]{1,0:T(8,128)(2,1)} %get-tuple-element.8.coupled_ref, bf16[8,128,128]{2,1,0:T(8,128)(2,1)} %dynamic-slice_bitcast_fusion.1.p_ref, f32[8,128,128]{2,1,0:T(8,128)} %fusion.2.sq_ref), custom_call_target="tpu_custom_call" | custom-call | flops 2500000000 | bytes 100000000 | tf_op jit(solution)/shard_map/pallas_call | solution.py:301
  201.8 1.5 select_reduce_fusion.1
  203.9 0.9 select_add_fusion
  204.8 0.1 copy.13
  204.9 0.9 fusion.11
  205.7 11.7 %cholesky.18 = f32[128,128]{1,0:T(8,128)S(1)} custom-call(f32[128,128]{1,0:T(8,128)S(1)} %fusion.11), custom_call_target="Cholesky" | custom-call | tf_op jit(solution)/shard_map/jit(cholesky)/cholesky | solution.py:522
  217.5 0.6 compare_reduce_fusion
  218.1 0.7 fusion.8
  218.8 9.8 %custom-call.7 = f32[1,128,128]{1,2,0:T(8,128)S(1)} custom-call(f32[1,128,128]{2,1,0:T(8,128)S(1)} %fusion.8), custom_call_target="InvertDiagBlocksLowerTriangular" | custom-call | tf_op jit(solution)/shard_map/jit(_solve_triangular)/triangular_solve | solution.py:523
  228.6 0.9 fusion.9.refs_0_
  229.5 53.5 %shard_map.79 = (f32[8,128,128]{2,1,0:T(8,128)}, bf16[2048,1024]{1,0:T(8,128)(2,1)}) custom-call(f32[128,128]{1,0:T(8,128)} %fusion.9.refs_0_, f32[8,128,128]{2,1,0:T(8,128)} %get-tuple-element.10.refs_1_), custom_call_target="tpu_custom_call" | custom-call | flops 200000000 | bytes 40000000 | tf_op jit(solution)/shard_map/pallas_call | solution.py:389
  283.0 6.5 %copy.18 = bf16[2048,1024]{0,1:T(8,128)(2,1)} copy(bf16[2048,1024]{1,0:T(8,128)(2,1)} %get-tuple-element.12.refs_2_) | data formatting | bytes 8388608 | tf_op jit(solution)/shard_map/reshape | solution.py:526
  289.5 1.7 dynamic-slice_bitcast_fusion.refs_5_
  291.2 5.7 %fusion.4.refs_6_ = f32[8,128,128]{2,1,0:T(8,128)} fusion(bf16[2048,8,128]{0,2,1:T(8,128)(2,1)} %bitcast.33, bf16[1,8,2048,128]{3,2,1,0:T(8,128)(2,1)} %param.8), kind=kOutput, calls=%fused_computation.4 | convolution fusion | flops 536870912 | bytes 8912896 | tf_op jit(solution)/shard_map/nbr,bnt->nrt/dot_general | solution.py:525
  296.9 34.2 %all-gather.2.cloned.1.call-done.refs_4_ = bf16[8,4,2048,128]{3,2,1,0:T(8,128)(2,1)} async-done(((bf16[1,4,2048,128]{3,2,1,0:T(8,128)(2,1)}), bf16[8,4,2048,128]{3,2,1,0:T(8,128)(2,1)}) %all-gather.2.cloned.1.call-update) | async-done | bytes 16777232 | tf_op jit(solution)/shard_map/all_gather | solution.py:514
  331.0 0.0 copy-start.2
  331.0 45.2 %shard_map.80 = f32[8,128,128]{2,1,0:T(8,128)} custom-call(s32[8]{0:T(128)} %bitcast.40, bf16[4,2048,128]{2,1,0:T(8,128)(2,1)} %bitcast.36, bf16[2048,1024]{1,0:T(8,128)(2,1)} %get-tuple-element.12.refs_2_, f32[4,8,128,128]{3,2,1,0:T(8,128)} %get-tuple-element.13.refs_3_, bf16[8,4,2048,128]{3,2,1,0:T(8,128)(2,1)} %all-gather.2.cloned.1.call-done.refs_4_, ...), custom_call_target="tpu_custom_call" | custom-call | flops 4499999744 | bytes 100000000 | tf_op jit(solution)/shard_map/pallas_call | solution.py:483
  376.3 0.0 copy-done.2
  376.3 0.8 copy.21
  377.1 1.9 copy.22
  (1 shorter events, 0.0 us)
Async XLA Ops:
  7.2 323.9 %all-gather.2.cloned.1.call-start = ((), (), s32[]{:S(2)}) async-start(), calls=%async_computation | async-start | bytes 18874368 | tf_op jit(solution)/shard_map/all_gather | solution.py:514
  9.6 104.7 %copy-start = (bf16[1,8,2048,128]{3,2,1,0:T(8,128)(2,1)S(1)}, bf16[1,8,2048,128]{3,2,1,0:T(8,128)(2,1)}, u32[]{:S(2)}) copy-start(bf16[1,8,2048,128]{3,2,1,0:T(8,128)(2,1)} %param.9) | copy-start | bytes 12582916
  9.6 104.7 %copy-start.1 = (bf16[2048,128]{1,0:T(8,128)(2,1)S(1)}, bf16[2048,128]{1,0:T(8,128)(2,1)}, u32[]{:S(2)}) copy-start(bf16[2048,128]{1,0:T(8,128)(2,1)} %sketch_ref.1) | copy-start | bytes 1572868
  331.0 45.2 %copy-start.2 = (f32[8,128,128]{2,1,0:T(8,128)S(1)}, f32[8,128,128]{2,1,0:T(8,128)}, u32[]{:S(2)}) copy-start(f32[8,128,128]{2,1,0:T(8,128)} %get-tuple-element.11) | copy-start | bytes 1572868
Sparse Core Ops, SparseCore 0:
  10.3 320.6 all-gather.1

commit v2 on v0

v2 whole, which is shorter than its diff:
```python
import math

import jax
import jax.numpy as jnp
from jax import lax
from jax.experimental import pallas as pl
from jax.experimental.pallas import tpu as pltpu
from jax.sharding import PartitionSpec as P

MESH = pl.DeviceIdType.MESH
HIGHEST = lax.Precision.HIGHEST
F32 = jnp.float32
BF16 = jnp.bfloat16
VMEM_LIMIT = 61 * 1024 * 1024


def device(row, place):
    return {"rows": row, "inner": place}


def greet(partners, count):
    barrier = pltpu.get_barrier_semaphore()
    for row, place in partners:
        pl.semaphore_signal(barrier, inc=1, device_id=device(row, place), device_id_type=MESH)
    pl.semaphore_wait(barrier, count)


def remote(src, dst, send_sem, recv_sem, row, place):
    return pltpu.make_async_remote_copy(
        src_ref=src, dst_ref=dst, send_sem=send_sem, recv_sem=recv_sem,
        device_id=device(row, place), device_id_type=MESH,
    )


class Send:
    def __init__(self, src, dst, send_sem, recv_sem, row, place, is_self):
        self.far = remote(src, dst, send_sem, recv_sem, row, place)
        self.near = pltpu.make_async_copy(src, dst, recv_sem)
        self.is_self = is_self

    def start(self):
        @pl.when(jnp.logical_not(self.is_self))
        def _():
            self.far.start()

        @pl.when(self.is_self)
        def _():
            self.near.start()

    def wait_send(self):
        @pl.when(jnp.logical_not(self.is_self))
        def _():
            self.far.wait_send()


def arrived(ref, sem):
    pltpu.make_async_copy(ref, ref, sem).wait()


def dot(a, b, precision=None):
    return jnp.dot(a, b, preferred_element_type=F32, precision=precision)


def dot_t(a, b, precision=None):
    return lax.dot_general(
        a, b, (((0,), (0,)), ((), ())), preferred_element_type=F32, precision=precision
    )


def dot_nt(a, b, precision=None):
    return lax.dot_general(
        a, b, (((1,), (1,)), ((), ())), preferred_element_type=F32, precision=precision
    )

LOW, HIGH = pl.ds(0, 512), pl.ds(512, 512)
ORDER = [(1, 2), (1, 1), (1, 3), (1, 0), (0, 2), (0, 1), (0, 3), (0, 0)]


class Place:
    def __init__(self):
        self.row, self.me = lax.axis_index("rows"), lax.axis_index("inner")
        self.core = lax.rem(self.me, 2)
        self.chip = self.me // 2
        self.z, self.y = self.chip // 4, lax.rem(self.chip, 4)
        self.base = self.me - self.core
        self.sib = self.base + 1 - self.core

    def chip_at(self, dz, dy):
        return lax.rem(self.z + dz, 2) * 4 + lax.rem(self.y + dy, 4)

    def inner_at(self, dz, dy):
        return self.chip_at(dz, dy) * 2 + self.core

    def row_at(self, dx, dz):
        x, z = self.row // 2, lax.rem(self.row, 2)
        return lax.rem(x + dx, 4) * 2 + lax.rem(z + dz, 2)


def inverse_factor(gram, work, inv):
    order = gram.shape[0]
    strip = 16
    row_id = lax.broadcasted_iota(jnp.int32, (order, order), 0)
    col_id = lax.broadcasted_iota(jnp.int32, (order, order), 1)
    diagonal = row_id == col_id
    ridge = 1e-06 * jnp.sum(jnp.where(diagonal, gram, 0.0)) / order
    work[...] = gram + jnp.where(diagonal, ridge, 0.0)
    inv[...] = jnp.where(diagonal, 1.0, 0.0)
    within = lax.broadcasted_iota(jnp.int32, (strip, order), 0)
    for lo in range(0, order, strip):
        a, m = work[lo : lo + strip, :], inv[lo : lo + strip, :]
        for j in range(strip):
            scale = lax.rsqrt(a[j : j + 1, lo + j : lo + j + 1])
            a_row, m_row = a[j : j + 1, :] * scale, m[j : j + 1, :] * scale
            factor = jnp.where(within > j, a[:, lo + j : lo + j + 1] * scale, 0.0)
            a = jnp.where(within == j, a_row, a - factor * a_row)
            m = jnp.where(within == j, m_row, m - factor * m_row)
        inv[lo : lo + strip, :] = m
        rest = lo + strip
        if rest < order:
            update = dot_t(a, jnp.concatenate([a, m], axis=1), HIGHEST)
            work[rest:, :] = work[rest:, :] - update[rest:, :order]
            inv[rest:, :] = inv[rest:, :] - update[rest:, order:]


class Reduction:
    def __init__(self, at, part, sibbuf, wire, hops, last, sems):
        self.at, self.part, self.sibbuf = at, part, sibbuf
        self.wire, self.hops, self.last = wire, hops, last
        self.i_send, self.i_recv, self.send, self.recv = sems
        self.copies, self.inner = [], []

    def own(self, n):
        return self.part.at[n, self.at.core]

    def offer(self, n):
        at = self.at
        copy = remote(
            self.part.at[n, 1 - at.core], self.sibbuf.at[n],
            self.i_send.at[n], self.i_recv.at[n], at.row, at.sib,
        )
        copy.start()
        self.inner.append(copy)

    def merge(self, n):
        self.inner[n].wait_recv()
        own = self.own(n)
        own[...] = own[...] + self.sibbuf[n]

    def hop(self, n, half, s, kind, way):
        at = self.at
        if self.wire is None:
            source = self.part.at[n, at.core, :, half]
        else:
            source = self.wire.at[pl.ds(n * 128, 128), half]
            source[...] = self.own(n)[:, half].astype(source.dtype)
        slot = (s * 3 + kind) * 2 + way
        to = at.inner_at(0, 1 if way == 0 else 3)
        copy = remote(source, self.hops.at[slot], self.send.at[slot], self.recv.at[slot], at.row, to)
        copy.start()
        self.copies.append(copy)

    def took(self, s, kind, way):
        slot = (s * 3 + kind) * 2 + way
        arrived(self.hops.at[slot], self.recv.at[slot])
        return self.hops[slot].astype(F32)

    def act(self, n):
        s, dy = ORDER[n]
        self.merge(n)
        if dy == 2:
            self.hop(n, LOW, s, 0, 0)
            self.hop(n, HIGH, s, 0, 1)
        elif dy == 1:
            self.hop(n, HIGH, s, 1, 0)
        elif dy == 3:
            self.hop(n, LOW, s, 1, 1)

    def relay(self, s):
        first = 4 * (1 - s)
        for n, half, way in ((first + 1, LOW, 0), (first + 2, HIGH, 1)):
            own = self.own(n)
            own[:, half] = own[:, half] + self.took(s, 0, way)
            self.hop(n, half, s, 2, way)

    def finish(self, s):
        own = self.own(4 * (1 - s) + 3)
        for half, kinds in ((LOW, (2, 1)), (HIGH, (1, 2))):
            own[:, half] = own[:, half] + self.took(s, kinds[0], 0) + self.took(s, kinds[1], 1)
        if s == 1:
            at = self.at
            copy = remote(
                own, self.last, self.send.at[12], self.recv.at[12], at.row, at.inner_at(1, 0)
            )
            copy.start()
            self.copies.append(copy)

    def total(self):
        arrived(self.last, self.recv.at[12])
        return self.own(7)[...] + self.last[...]

    def run(self, compute, between=None):
        for n in range(8):
            compute(n)
            self.offer(n)
            if 1 <= n <= 4:
                self.act(n - 1)
        self.relay(1)
        for n in range(4, 8):
            self.act(n)
        self.finish(1)
        self.relay(0)
        if between is not None:
            between()
        self.finish(0)
        return self.total()

    def wait_sends(self):
        for copy in self.inner + self.copies:
            copy.wait_send()


def update_kernel(
    scale, cols_ref, u_ref, v_ref, p_ref, q_ref, sketch_ref, left_ref, right_ref,
    panel, vbuf, sown, sbuf, gown, gsib, cown, coupled, coupling,
    tiles, mid, p_rows, q_rows, part, sibbuf, d_hops, d_last, r_hops, r_last,
    sample, dsum, gpart, grbuf, work, inv, lbuf, bown, basis, ib,
    local, v_send, v_recv, s_send, s_recv, g_send, g_recv, c_send, c_recv, k_send, k_recv,
    u_send, u_recv, di_send, di_recv, d_send, d_recv, gr_send, gr_recv, l_send, l_recv,
    b_send, b_recv, bh_recv, f_send, f_recv, ri_send, ri_recv, r_send, r_recv,
):
    at = Place()
    row, me, core, base, sib = at.row, at.me, at.core, at.base, at.sib
    owner_core = row // 4
    slot = lax.rem(row, 4)
    my_rows = pl.ds(pl.multiple_of(me * 128, 128), 128)

    own_u = pltpu.make_async_copy(u_ref, panel.at[row], local.at[0])
    own_u.start()
    load_p = pltpu.make_async_copy(p_ref.at[:, my_rows, :], p_rows, local.at[1])
    load_p.start()
    load_q = pltpu.make_async_copy(q_ref.at[:, my_rows, :], q_rows, local.at[2])
    load_q.start()
    load_tiles = pltpu.make_async_copy(q_ref.at[pl.ds(0, 4)], tiles, local.at[3])
    load_tiles.start()

    partners = [(lax.rem(row + d, 8), base + h) for d in range(1, 8) for h in range(2)]
    partners += [(row, lax.rem(me + d, 16)) for d in range(1, 16)]
    greet(partners, len(partners))

    v_copies = []
    for n in range(8):
        kk, hh = lax.rem(slot + n // 2, 4), lax.rem(n + core, 2)
        to = core * 4 + kk
        copy = Send(
            v_ref.at[kk, pl.ds(pl.multiple_of(hh * 1024, 1024), 1024), :],
            vbuf.at[:, pl.ds(pl.multiple_of(row * 128, 128), 128)],
            v_send.at[n], v_recv.at[row], to, base + hh,
            jnp.logical_and(to == row, core == hh),
        )
        copy.start()
        v_copies.append(copy)

    s_copies = []
    own_u.wait()
    for kk in range(4):
        sown[kk] = dot_t(panel[row, kk], sketch_ref[...])
        to = core * 4 + kk
        copy = Send(
            sown.at[kk], sbuf.at[slot], s_send.at[kk], s_recv.at[slot],
            to, base + owner_core, jnp.logical_and(to == row, core == owner_core),
        )
        copy.start()
        s_copies.append(copy)

    load_tiles.wait()
    for c in range(4):
        mid[c] = dot_t(tiles[c], sketch_ref[...])
    load_tiles = pltpu.make_async_copy(q_ref.at[pl.ds(4, 4)], tiles, local.at[3])
    load_tiles.start()
    load_tiles.wait()
    for c in range(4):
        mid[4 + c] = dot_t(tiles[c], sketch_ref[...])
    load_p.wait()
    for c in range(8):
        sample[c] = dot(p_rows[c].astype(F32), mid[c], HIGHEST)
    load_tiles = pltpu.make_async_copy(p_ref.at[pl.ds(0, 4)], tiles, local.at[3])
    load_tiles.start()

    for i in range(8):
        arrived(vbuf.at[:, pl.ds(i * 128, 128)], v_recv.at[i])

    u_copies = []

    def pass_panel(index, piece, dx, dz):
        ref = panel.at[index] if piece is None else panel.at[index, pl.ds(piece * 2, 2)]
        n = len(u_copies)
        copy = remote(ref, ref, u_send.at[n], u_recv.at[n], at.row_at(dx, dz), me)
        copy.start()
        u_copies.append(copy)

    def panel_here(n, index, piece=None):
        ref = panel.at[index] if piece is None else panel.at[index, pl.ds(piece * 2, 2)]
        arrived(ref, u_recv.at[n])

    pass_panel(row, None, 1, 0)
    pass_panel(row, None, 3, 0)
    pass_panel(row, None, 0, 1)

    def gram_half(half, write):
        right = vbuf[:, pl.ds(pl.multiple_of(half * 512, 512), 512)]
        for pair in range(4):
            value = dot_t(vbuf[:, pl.ds(pair * 256, 256)], right)
            for p in range(2):
                write(pair * 2 + p, value[p * 128 : p * 128 + 128])

    def write_out(i, value):
        part[i, 0, :, :512] = value

    def write_own(i, value):
        for j in range(4):
            gown[i, j] = value[:, j * 128 : j * 128 + 128]

    gram_half(1 - core, write_out)
    g_copy = remote(part.at[:, 0, :, LOW], gsib, g_send, g_recv, row, sib)
    g_copy.start()
    gram_half(core, write_own)
    g_copy.wait_recv()
    for j in range(4):
        arrived(sbuf.at[j], s_recv.at[j])
    c_copies = []
    for i in range(8):
        for j in range(4):
            total = gown[i, j] + gsib[i, :, j * 128 : j * 128 + 128]
            gown[i, j] = total
            cown[i * 128 : i * 128 + 128, j * 128 : j * 128 + 128] = dot(
                total, sbuf[j], HIGHEST
            ).astype(BF16)
        copy = Send(
            cown.at[pl.ds(i * 128, 128), :],
            coupled.at[
                pl.ds(pl.multiple_of(slot * 128, 128), 128),
                pl.ds(pl.multiple_of(core * 512, 512), 512),
            ],
            c_send.at[i], c_recv.at[slot * 2 + core], i, base + owner_core,
            jnp.logical_and(row == i, core == owner_core),
        )
        copy.start()
        c_copies.append(copy)
    for kk in range(4):
        for hh in range(2):
            arrived(
                coupled.at[pl.ds(kk * 128, 128), pl.ds(hh * 512, 512)], c_recv.at[kk * 2 + hh]
            )
    for i in range(8):
        copy = Send(
            gown.at[i], coupling.at[slot, pl.ds(core * 4, 4)],
            k_send.at[i], k_recv.at[slot * 2 + core], i, base + owner_core,
            jnp.logical_and(row == i, core == owner_core),
        )
        copy.start()
        c_copies.append(copy)
    g_copy.wait_send()

    def panel_block(n, index):
        rows = pl.ds(pl.multiple_of(at.chip_at(*ORDER[n]) * 256, 256), 256)
        return jnp.concatenate([panel[index, kk, rows, :] for kk in range(4)], axis=1)

    def d_block(n):
        value = dot(panel_block(n, row), coupled[...])
        part[n, 0] = value[:128]
        part[n, 1] = value[128:]

    def second_leg():
        panel_here(0, at.row_at(3, 0))
        panel_here(1, at.row_at(1, 0))
        pass_panel(at.row_at(3, 0), 0, 1, 0)
        pass_panel(at.row_at(1, 0), 1, 3, 0)
        panel_here(2, at.row_at(0, 1))
        pass_panel(at.row_at(0, 1), None, 1, 0)
        pass_panel(at.row_at(0, 1), None, 3, 0)

    reduction = Reduction(
        at, part, sibbuf, None, d_hops, d_last, (di_send, di_recv, d_send, d_recv)
    )
    total = reduction.run(d_block)
    for j in range(8):
        dsum[j] = total[:, j * 128 : j * 128 + 128]

    gram_copies = []
    for c in range(8):
        value = sample[c] - dsum[cols_ref[c]]
        sample[c] = value
        gpart[c] = dot_t(value, value, HIGHEST)
        for h in range(2):
            copy = Send(
                gpart.at[c], grbuf.at[me], gr_send.at[c * 2 + h], gr_recv.at[me],
                row, c * 2 + h, me == c * 2 + h,
            )
            copy.start()
            gram_copies.append(copy)
    second_leg()
    gram = jnp.zeros((128, 128), F32)
    for m in range(16):
        arrived(grbuf.at[m], gr_recv.at[m])
        gram = gram + grbuf[m]
    inverse_factor(gram, work, inv)

    l_copies = []
    for n, step in enumerate(ORDER[:7]):
        copy = remote(
            inv, lbuf.at[at.chip], l_send.at[n], l_recv.at[at.chip], row, at.inner_at(*step)
        )
        copy.start()
        l_copies.append(copy)
    lbuf[at.chip] = inv[...]
    panel_here(3, at.row_at(2, 0), 0)
    panel_here(4, at.row_at(2, 0), 1)
    pass_panel(at.row_at(2, 0), None, 0, 1)
    for step in ORDER[:7]:
        source = at.chip_at(*step)
        arrived(lbuf.at[source], l_recv.at[source])
    for c in range(8):
        value = dot_nt(sample[c], lbuf[c], HIGHEST)
        left_ref[c] = value * scale
        bown[:, c * 128 : c * 128 + 128] = value.astype(BF16)

    b_copies, f_copies = [], []

    def block(m, half=None):
        rows = pl.ds(pl.multiple_of(m * 128, 128), 128)
        return basis.at[rows, :] if half is None else basis.at[rows, half]

    def pass_basis(source, dest, recv, dz, dy):
        copy = remote(source, dest, b_send.at[len(b_copies)], recv, row, at.inner_at(dz, dy))
        copy.start()
        b_copies.append(copy)

    def to_sib(source, dest, n):
        copy = remote(source, dest, f_send.at[n], f_recv.at[n], row, sib)
        copy.start()
        f_copies.append(copy)

    pass_basis(bown, block(me), b_recv.at[0], 1, 0)
    pass_basis(bown, block(me), b_recv.at[1], 0, 1)
    pass_basis(bown, block(me), b_recv.at[2], 0, 3)
    to_sib(bown, block(me), 0)
    basis[my_rows, :] = bown[...]
    other = at.inner_at(1, 0)
    arrived(block(other), b_recv.at[0])
    pass_basis(block(other), block(other), b_recv.at[3], 0, 1)
    pass_basis(block(other), block(other), b_recv.at[4], 0, 3)
    to_sib(block(other), block(other), 1)
    for s in range(2):
        for way, dy in ((0, 3), (1, 1)):
            m = at.inner_at(s, dy)
            half = HIGH if way else LOW
            n = 1 + s * 2 + way
            arrived(block(m), b_recv.at[n])
            pass_basis(block(m, half), block(m, half), bh_recv.at[s * 2 + way], 0, 3 if way else 1)
            to_sib(block(m), block(m), 1 + n)
    reduction.wait_sends()

    def basis_term(n, dz, dy, first=False):
        chip = at.chip_at(dz, dy)
        if n < 6:
            m = chip * 2 + 1 - core
            arrived(block(m), f_recv.at[n])
        rows = pl.ds(pl.multiple_of(chip * 256, 256), 256)
        for kk in range(4):
            for h in range(2):
                value = dot_t(panel[row, kk, rows, :], basis[rows, h * 512 : h * 512 + 512])
                gsib[kk * 2 + h] = value if first else gsib[kk * 2 + h] + value

    basis_term(0, 0, 0, True)
    basis_term(1, 1, 0)
    basis_term(2, 0, 3)
    basis_term(3, 0, 1)
    basis_term(4, 1, 3)
    basis_term(5, 1, 1)
    for s in range(2):
        m = at.inner_at(s, 2)
        for way in range(2):
            half = HIGH if way else LOW
            arrived(block(m, half), bh_recv.at[s * 2 + way])
            to_sib(block(m, half), block(m, half), 6 + s * 2 + way)
    for s in range(2):
        m = at.chip_at(s, 2) * 2 + 1 - core
        for way in range(2):
            arrived(block(m, HIGH if way else LOW), f_recv.at[6 + s * 2 + way])
        basis_term(6 + s, s, 2)

    for kk in range(4):
        for hh in range(2):
            arrived(coupling.at[kk, pl.ds(hh * 4, 4)], k_recv.at[kk * 2 + hh])
    for kk in range(4):
        for c in range(8):
            lanes = pl.ds((c % 4) * 128, 128)
            ib[kk * 128 : kk * 128 + 128, c * 128 : c * 128 + 128] = dot_t(
                coupling[kk, cols_ref[c]], gsib[kk * 2 + c // 4, :, lanes], HIGHEST
            ).astype(BF16)
    panel_here(5, at.row_at(3, 1))
    panel_here(6, at.row_at(1, 1))
    panel_here(7, at.row_at(2, 1))

    def r_block(n):
        for c in range(8):
            value = dot(panel_block(n, cols_ref[c]), ib[:, c * 128 : c * 128 + 128])
            part[n, 0, :, c * 128 : c * 128 + 128] = value[:128]
            part[n, 1, :, c * 128 : c * 128 + 128] = value[128:]

    def p_basis():
        for t in range(2):
            if t == 1:
                again = pltpu.make_async_copy(p_ref.at[pl.ds(4, 4)], tiles, local.at[3])
                again.start()
                again.wait()
            for c in range(4):
                n = t * 4 + c
                mid[n] = dot_t(tiles[c], basis[:, n * 128 : n * 128 + 128])
        for c in range(8):
            sample[c] = dot(q_rows[c].astype(F32), mid[c], HIGHEST)

    load_tiles.wait()
    load_q.wait()
    projection = Reduction(
        at, part, sibbuf, vbuf, r_hops, r_last, (ri_send, ri_recv, r_send, r_recv)
    )
    total = projection.run(r_block, p_basis)
    for c in range(8):
        right_ref[c] = (sample[c] - total[:, c * 128 : c * 128 + 128]) * (1.0 / scale)

    for copy in v_copies + s_copies + c_copies + u_copies + gram_copies + l_copies:
        copy.wait_send()
    for copy in b_copies + f_copies:
        copy.wait_send()
    projection.wait_sends()


def update(u, v, p, q, sketch, cols, scale):
    dma = pltpu.SemaphoreType.DMA
    vmem = pl.BlockSpec(memory_space=pltpu.VMEM)
    smem = pl.BlockSpec(memory_space=pltpu.SMEM)
    hbm = pl.BlockSpec(memory_space=pl.ANY)

    def kernel(*refs):
        update_kernel(scale, *refs)

    squares = jax.ShapeDtypeStruct((8, 128, 128), F32)
    return pl.pallas_call(
        kernel,
        out_shape=(squares, squares),
        in_specs=[smem, hbm, hbm, hbm, hbm, vmem],
        out_specs=(vmem, vmem),
        scratch_shapes=[
            pltpu.VMEM((8, 4, 2048, 128), BF16),
            pltpu.VMEM((1024, 1024), BF16),
            pltpu.VMEM((4, 128, 128), F32),
            pltpu.VMEM((4, 128, 128), F32),
            pltpu.VMEM((8, 4, 128, 128), F32),
            pltpu.VMEM((8, 128, 512), F32),
            pltpu.VMEM((1024, 512), BF16),
            pltpu.VMEM((512, 1024), BF16),
            pltpu.VMEM((4, 8, 128, 128), F32),
            pltpu.VMEM((4, 2048, 128), BF16),
            pltpu.VMEM((8, 128, 128), F32),
            pltpu.VMEM((8, 128, 128), BF16),
            pltpu.VMEM((8, 128, 128), BF16),
            pltpu.VMEM((8, 2, 128, 1024), F32),
            pltpu.VMEM((8, 128, 1024), F32),
            pltpu.VMEM((12, 128, 512), F32),
            pltpu.VMEM((128, 1024), F32),
            pltpu.VMEM((12, 128, 512), BF16),
            pltpu.VMEM((128, 1024), F32),
            pltpu.VMEM((8, 128, 128), F32),
            pltpu.VMEM((8, 128, 128), F32),
            pltpu.VMEM((8, 128, 128), F32),
            pltpu.VMEM((16, 128, 128), F32),
            pltpu.VMEM((128, 128), F32),
            pltpu.VMEM((128, 128), F32),
            pltpu.VMEM((8, 128, 128), F32),
            pltpu.VMEM((128, 1024), BF16),
            pltpu.VMEM((2048, 1024), BF16),
            pltpu.VMEM((512, 1024), BF16),
            dma((4,)), dma((8,)), dma((8,)), dma((4,)), dma((4,)), dma, dma,
            dma((8,)), dma((8,)), dma((8,)), dma((8,)),
            dma((8,)), dma((8,)), dma((8,)), dma((8,)), dma((13,)), dma((13,)),
            dma((16,)), dma((16,)), dma((7,)), dma((8,)),
            dma((9,)), dma((5,)), dma((4,)), dma((10,)), dma((10,)),
            dma((8,)), dma((8,)), dma((13,)), dma((13,)),
        ],
        compiler_params=pltpu.CompilerParams(
            collective_id=1, has_side_effects=True, vmem_limit_bytes=VMEM_LIMIT
        ),
        cost_estimate=pl.CostEstimate(
            flops=13_000_000_000, bytes_accessed=30_000_000, transcendentals=0
        ),
    )(cols, u, v, p, q, sketch)


def body(left_u, left_v, tile_p, tile_q, sketch, tile_cols):
    factor_scale = math.sqrt(sketch.shape[0])
    new_left, new_right = update(
        left_u[0], left_v[0], tile_p[0], tile_q[0], sketch, tile_cols[0], factor_scale
    )
    return new_left[None], new_right[None]


def solution(mesh):
    return jax.shard_map(
        body,
        mesh=mesh,
        in_specs=(
            P("rows", "inner", None, None),
            P("rows", "inner", None, None),
            P("rows", None, None, None),
            P("rows", None, None, None),
            P(),
            P("rows", None),
        ),
        out_specs=(P("rows", None, "inner", None), P("rows", None, "inner", None)),
        check_vma=False,
    )
```

time: 1030 us -> 277 us (0.27)
  waiting for transfers between devices: 577 us -> 0 us
  Pallas kernels: 0 us -> 268 us
  other arithmetic: 179 us -> 0 us
  matrix products: 159 us -> 0 us
  loops' own time: 72.5 us -> 0 us
  local copies, waits for them, and re-layouts: 21.9 us -> 3.74 us
  between operations: 13.9 us -> 0.64 us
    all_gather x2 -> x0, waiting for transfers between devices: 377 us -> none  [the longest x1 190 us: body(): lax.all_gather(left_u, 'rows', axis=0, tiled=True)]
    pallas_call x0 -> x1, Pallas kernels: none -> 268 us  [update(): pl.pallas_call(kernel, out_shape=(squares, squares), in_specs=[smem, hbm,...]
    another operation x9 -> x0, other arithmetic: 173 us -> none  [the longest x4 94.7 us: from_gram(): triangle = jnp.linalg.cholesky(gram)]
    dot_general x61 -> x0, matrix products: 149 us -> none  [the longest x8 29.6 us: partial_sample(): jnp.einsum('kbr,kbs->krs', left_v[row_id], gathered_v[column], preferred_...]
    psum x1 -> x0, waiting for transfers between devices: 137 us -> none  [body(): sample_sum = lax.psum(samples, 'inner')]
    another operation x2 -> x0, loops' own time: 72.5 us -> none  [the longest x1 41.1 us: body(): rights = lax.map(partial_right, targets)]
    reduce_scatter x1 -> x0, waiting for transfers between devices: 62.3 us -> none  [body(): lax.psum_scatter(rights, 'inner', scatter_dimension=1, tiled=True)]
    dynamic_slice x32 -> x0, local copies, waits for them, and re-layouts: 19.1 us -> none  [the longest x16 9.32 us: body(): samples, couplings = lax.map(partial_sample, targets)]
  transfers between devices with their start and end apart: 4 -> 0, of which waited for: 4 -> 0; matrix products, arithmetic and copies ran while one was open for 1% -> 0% of each run, Pallas kernels for 0% -> 0%
where the time goes in v2:
time: 277 us; the launch traced here: 272 us
  Pallas kernels  268 us (97%)
  local copies, waits for them, and re-layouts  3.74 us (1%)
    pallas_call x1, Pallas kernels, update(): pl.pallas_call(kernel, out_shape=(squares, squares), in_specs=[smem, hbm,...  268 us

profile of v2, /device:TPU:1, one launch (start us, length us, event | category | flops | bytes accessed | tf_op | source)
XLA Modules:
  0.0 272.0 jit_solution(16689544532730874241)
XLA Ops:
  0.6 267.6 %shard_map.77 = (f32[8,128,128]{2,1,0:T(8,128)}, f32[8,128,128]{2,1,0:T(8,128)}) custom-call(s32[8]{0:T(128)} %bitcast.13, bf16[4,2048,128]{2,1,0:T(8,128)(2,1)} %bitcast.11, bf16[4,2048,128]{2,1,0:T(8,128)(2,1)} %bitcast.12, bf16[8,2048,128]{2,1,0:T(8,128)(2,1)} %bitcast.9, bf16[8,2048,128]{2,1,0:T(8,128)(2,1)} %bitcast.10, bf16[2048,128]{1,0:T(8,128)(2,1)} %refs_5_.1), custom_call_target="tpu_custom_call" | custom-call | flops 12999999488 | bytes 30000000 | tf_op jit(solution)/shard_map/pallas_call | solution.py:549
  268.2 1.9 copy.10
  270.1 1.9 copy.11

commit v3 on v2

--- a/solution.py
+++ b/solution.py
@@ -74,6 +74,10 @@
 
 LOW, HIGH = pl.ds(0, 512), pl.ds(512, 512)
 ORDER = [(1, 2), (1, 1), (1, 3), (1, 0), (0, 2), (0, 1), (0, 3), (0, 0)]
+
+
+def position(n):
+    return ORDER[n][0] * 4 + ORDER[n][1]
 
 
 class Place:
@@ -130,12 +134,12 @@
         self.copies, self.inner = [], []
 
     def own(self, n):
-        return self.part.at[n, self.at.core]
+        return self.part.at[position(n), self.at.core]
 
     def offer(self, n):
         at = self.at
         copy = remote(
-            self.part.at[n, 1 - at.core], self.sibbuf.at[n],
+            self.part.at[position(n), 1 - at.core], self.sibbuf.at[n],
             self.i_send.at[n], self.i_recv.at[n], at.row, at.sib,
         )
         copy.start()
@@ -149,7 +153,7 @@
     def hop(self, n, half, s, kind, way):
         at = self.at
         if self.wire is None:
-            source = self.part.at[n, at.core, :, half]
+            source = self.part.at[position(n), at.core, :, half]
         else:
             source = self.wire.at[pl.ds(n * 128, 128), half]
             source[...] = self.own(n)[:, half].astype(source.dtype)
@@ -196,7 +200,9 @@
 
     def total(self):
         arrived(self.last, self.recv.at[12])
-        return self.own(7)[...] + self.last[...]
+        own = self.own(7)
+        own[...] = own[...] + self.last[...]
+        return own
 
     def run(self, compute, between=None):
         for n in range(8):
@@ -227,6 +233,7 @@
     local, v_send, v_recv, s_send, s_recv, g_send, g_recv, c_send, c_recv, k_send, k_recv,
     u_send, u_recv, di_send, di_recv, d_send, d_recv, gr_send, gr_recv, l_send, l_recv,
     b_send, b_recv, bh_recv, f_send, f_recv, ri_send, ri_recv, r_send, r_recv,
+    u_own, their_cols, swapped, cols_sem, i_send, i_recv, t_send, t_recv,
 ):
     at = Place()
     row, me, core, base, sib = at.row, at.me, at.core, at.base, at.sib
@@ -234,8 +241,12 @@
     slot = lax.rem(row, 4)
     my_rows = pl.ds(pl.multiple_of(me * 128, 128), 128)
 
-    own_u = pltpu.make_async_copy(u_ref, panel.at[row], local.at[0])
+    half_z = lax.rem(row, 2)
+    partner = at.row_at(0, 1)
+    own_u = pltpu.make_async_copy(u_ref, u_own, local.at[0])
     own_u.start()
+    start_panel = pltpu.make_async_copy(u_ref.at[:, :, half_z], panel.at[row], local.at[4])
+    start_panel.start()
     load_p = pltpu.make_async_copy(p_ref.at[:, my_rows, :], p_rows, local.at[1])
     load_p.start()
     load_q = pltpu.make_async_copy(q_ref.at[:, my_rows, :], q_rows, local.at[2])
@@ -246,6 +257,8 @@
     partners = [(lax.rem(row + d, 8), base + h) for d in range(1, 8) for h in range(2)]
     partners += [(row, lax.rem(me + d, 16)) for d in range(1, 16)]
     greet(partners, len(partners))
+    cols_copy = remote(cols_ref, their_cols, cols_sem.at[0], cols_sem.at[1], partner, me)
+    cols_copy.start()
 
     v_copies = []
     for n in range(8):
@@ -263,7 +276,7 @@
     s_copies = []
     own_u.wait()
     for kk in range(4):
-        sown[kk] = dot_t(panel[row, kk], sketch_ref[...])
+        sown[kk] = dot_t(u_own[kk].reshape(2048, 128), sketch_ref[...])
         to = core * 4 + kk
         copy = Send(
             sown.at[kk], sbuf.at[slot], s_send.at[kk], s_recv.at[slot],
@@ -288,23 +301,6 @@
 
     for i in range(8):
         arrived(vbuf.at[:, pl.ds(i * 128, 128)], v_recv.at[i])
-
-    u_copies = []
-
-    def pass_panel(index, piece, dx, dz):
-        ref = panel.at[index] if piece is None else panel.at[index, pl.ds(piece * 2, 2)]
-        n = len(u_copies)
-        copy = remote(ref, ref, u_send.at[n], u_recv.at[n], at.row_at(dx, dz), me)
-        copy.start()
-        u_copies.append(copy)
-
-    def panel_here(n, index, piece=None):
-        ref = panel.at[index] if piece is None else panel.at[index, pl.ds(piece * 2, 2)]
-        arrived(ref, u_recv.at[n])
-
-    pass_panel(row, None, 1, 0)
-    pass_panel(row, None, 3, 0)
-    pass_panel(row, None, 0, 1)
 
     def gram_half(half, write):
         right = vbuf[:, pl.ds(pl.multiple_of(half * 512, 512), 512)]
@@ -361,23 +357,46 @@
         c_copies.append(copy)
     g_copy.wait_send()
 
-    def panel_block(n, index):
-        rows = pl.ds(pl.multiple_of(at.chip_at(*ORDER[n]) * 256, 256), 256)
-        return jnp.concatenate([panel[index, kk, rows, :] for kk in range(4)], axis=1)
+    u_copies = []
+
+    def pass_panel(index, piece, dx, dz):
+        ref = panel.at[index] if piece is None else panel.at[index, pl.ds(piece * 2, 2)]
+        n = len(u_copies)
+        copy = remote(ref, ref, u_send.at[n], u_recv.at[n], at.row_at(dx, dz), me)
+        copy.start()
+        u_copies.append(copy)
+
+    def panel_here(n, index, piece=None):
+        ref = panel.at[index] if piece is None else panel.at[index, pl.ds(piece * 2, 2)]
+        arrived(ref, u_recv.at[n])
+
+    start_panel.wait()
+    give = u_own.at[:, :, 1 - half_z]
+    copy = remote(give, panel.at[row], u_send.at[0], u_recv.at[0], partner, me)
+    copy.start()
+    u_copies.append(copy)
+    pass_panel(row, None, 1, 0)
+    pass_panel(row, None, 3, 0)
 
     def d_block(n):
-        value = dot(panel_block(n, row), coupled[...])
-        part[n, 0] = value[:128]
-        part[n, 1] = value[128:]
+        chip = at.chip_at(*ORDER[n])
+        left = jnp.concatenate([u_own[kk, chip].reshape(256, 128) for kk in range(4)], axis=1)
+        value = dot(left, coupled[...])
+        part[position(n), 0] = value[:128]
+        part[position(n), 1] = value[128:]
 
     def second_leg():
-        panel_here(0, at.row_at(3, 0))
-        panel_here(1, at.row_at(1, 0))
-        pass_panel(at.row_at(3, 0), 0, 1, 0)
-        pass_panel(at.row_at(1, 0), 1, 3, 0)
-        panel_here(2, at.row_at(0, 1))
-        pass_panel(at.row_at(0, 1), None, 1, 0)
-        pass_panel(at.row_at(0, 1), None, 3, 0)
+        panel_here(0, partner)
+        pass_panel(partner, None, 1, 0)
+        pass_panel(partner, None, 3, 0)
+        for n, dx in ((1, 3), (2, 1)):
+            panel_here(n, at.row_at(dx, 0))
+            pass_panel(at.row_at(dx, 0), n - 1, 4 - dx, 0)
+
+    def third_leg():
+        for n, dx in ((3, 3), (4, 1)):
+            panel_here(n, at.row_at(dx, 1))
+            pass_panel(at.row_at(dx, 1), n - 3, 4 - dx, 0)
 
     reduction = Reduction(
         at, part, sibbuf, None, d_hops, d_last, (di_send, di_recv, d_send, d_recv)
@@ -413,9 +432,7 @@
         copy.start()
         l_copies.append(copy)
     lbuf[at.chip] = inv[...]
-    panel_here(3, at.row_at(2, 0), 0)
-    panel_here(4, at.row_at(2, 0), 1)
-    pass_panel(at.row_at(2, 0), None, 0, 1)
+    third_leg()
     for step in ORDER[:7]:
         source = at.chip_at(*step)
         arrived(lbuf.at[source], l_recv.at[source])
@@ -468,7 +485,7 @@
         rows = pl.ds(pl.multiple_of(chip * 256, 256), 256)
         for kk in range(4):
             for h in range(2):
-                value = dot_t(panel[row, kk, rows, :], basis[rows, h * 512 : h * 512 + 512])
+                value = dot_t(u_own[kk, chip].reshape(256, 128), basis[rows, h * 512 : h * 512 + 512])
                 gsib[kk * 2 + h] = value if first else gsib[kk * 2 + h] + value
 
     basis_term(0, 0, 0, True)
@@ -492,21 +509,45 @@
     for kk in range(4):
         for hh in range(2):
             arrived(coupling.at[kk, pl.ds(hh * 4, 4)], k_recv.at[kk * 2 + hh])
+    i_copies = []
     for kk in range(4):
         for c in range(8):
             lanes = pl.ds((c % 4) * 128, 128)
-            ib[kk * 128 : kk * 128 + 128, c * 128 : c * 128 + 128] = dot_t(
+            ib[half_z, kk * 128 : kk * 128 + 128, c * 128 : c * 128 + 128] = dot_t(
                 coupling[kk, cols_ref[c]], gsib[kk * 2 + c // 4, :, lanes], HIGHEST
             ).astype(BF16)
-    panel_here(5, at.row_at(3, 1))
-    panel_here(6, at.row_at(1, 1))
-    panel_here(7, at.row_at(2, 1))
+        ref = ib.at[half_z, pl.ds(kk * 128, 128), :]
+        copy = remote(ref, ref, i_send.at[kk], i_recv.at[kk], partner, me)
+        copy.start()
+        i_copies.append(copy)
+    panel_here(5, at.row_at(2, 0), 0)
+    panel_here(6, at.row_at(2, 0), 1)
+    panel_here(7, at.row_at(2, 1), 0)
+    panel_here(8, at.row_at(2, 1), 1)
+
+    def terms(s, which, cols):
+        chips = pl.ds(pl.multiple_of(lax.rem(at.z + s, 2) * 4, 4), 4)
+        for c in range(8):
+            lanes = pl.ds(c * 128, 128)
+            col = cols[c]
+            left = jnp.concatenate(
+                [panel[col, kk, chips].reshape(512, 128) for kk in range(4)], axis=1
+            )
+            value = dot(left, ib[which, :, lanes])
+            for y in range(4):
+                part[s * 4 + lax.rem(y + 4 - at.y, 4), which, :, lanes] = value[
+                    y * 128 : y * 128 + 128
+                ]
+
+    terms(1, half_z, cols_ref)
+    terms(0, half_z, cols_ref)
+    arrived(their_cols, cols_sem.at[1])
+    for kk in range(4):
+        arrived(ib.at[1 - half_z, pl.ds(kk * 128, 128), :], i_recv.at[kk])
 
     def r_block(n):
-        for c in range(8):
-            value = dot(panel_block(n, cols_ref[c]), ib[:, c * 128 : c * 128 + 128])
-            part[n, 0, :, c * 128 : c * 128 + 128] = value[:128]
-            part[n, 1, :, c * 128 : c * 128 + 128] = value[128:]
+        if n % 4 == 0:
+            terms(1 - n // 4, 1 - half_z, their_cols)
 
     def p_basis():
         for t in range(2):
@@ -526,12 +567,28 @@
         at, part, sibbuf, vbuf, r_hops, r_last, (ri_send, ri_recv, r_send, r_recv)
     )
     total = projection.run(r_block, p_basis)
-    for c in range(8):
-        right_ref[c] = (sample[c] - total[:, c * 128 : c * 128 + 128]) * (1.0 / scale)
-
+
+    def write_right(source):
+        for c in range(8):
+            right_ref[c] = (sample[c] - source[:, c * 128 : c * 128 + 128]) * (1.0 / scale)
+
+    swap = remote(total, swapped, t_send, t_recv, partner, sib)
+
+    @pl.when(core == half_z)
+    def _():
+        write_right(total)
+
+    @pl.when(core != half_z)
+    def _():
+        swap.start()
+        swap.wait_recv()
+        write_right(swapped)
+        swap.wait_send()
+
+    cols_copy.wait_send()
     for copy in v_copies + s_copies + c_copies + u_copies + gram_copies + l_copies:
         copy.wait_send()
-    for copy in b_copies + f_copies:
+    for copy in b_copies + f_copies + i_copies:
         copy.wait_send()
     projection.wait_sends()
 
@@ -552,7 +609,7 @@
         in_specs=[smem, hbm, hbm, hbm, hbm, vmem],
         out_specs=(vmem, vmem),
         scratch_shapes=[
-            pltpu.VMEM((8, 4, 2048, 128), BF16),
+            pltpu.VMEM((8, 4, 8, 128, 128), BF16),
             pltpu.VMEM((1024, 1024), BF16),
             pltpu.VMEM((4, 128, 128), F32),
             pltpu.VMEM((4, 128, 128), F32),
@@ -580,13 +637,17 @@
             pltpu.VMEM((8, 128, 128), F32),
             pltpu.VMEM((128, 1024), BF16),
             pltpu.VMEM((2048, 1024), BF16),
-            pltpu.VMEM((512, 1024), BF16),
-            dma((4,)), dma((8,)), dma((8,)), dma((4,)), dma((4,)), dma, dma,
+            pltpu.VMEM((2, 512, 1024), BF16),
+            dma((5,)), dma((8,)), dma((8,)), dma((4,)), dma((4,)), dma, dma,
             dma((8,)), dma((8,)), dma((8,)), dma((8,)),
-            dma((8,)), dma((8,)), dma((8,)), dma((8,)), dma((13,)), dma((13,)),
+            dma((9,)), dma((9,)), dma((8,)), dma((8,)), dma((13,)), dma((13,)),
             dma((16,)), dma((16,)), dma((7,)), dma((8,)),
             dma((9,)), dma((5,)), dma((4,)), dma((10,)), dma((10,)),
             dma((8,)), dma((8,)), dma((13,)), dma((13,)),
+            pltpu.VMEM((4, 8, 2, 128, 128), BF16),
+            pltpu.SMEM((8,), jnp.int32),
+            pltpu.VMEM((128, 1024), F32),
+            dma((2,)), dma((4,)), dma((4,)), dma, dma,
         ],
         compiler_params=pltpu.CompilerParams(
             collective_id=1, has_side_effects=True, vmem_limit_bytes=VMEM_LIMIT
@@ -600,7 +661,7 @@
 def body(left_u, left_v, tile_p, tile_q, sketch, tile_cols):
     factor_scale = math.sqrt(sketch.shape[0])
     new_left, new_right = update(
-        left_u[0], left_v[0], tile_p[0], tile_q[0], sketch, tile_cols[0], factor_scale
+        left_u[0].reshape(4, 8, 2, 128, 128), left_v[0], tile_p[0], tile_q[0], sketch, tile_cols[0], factor_scale
     )
     return new_left[None], new_right[None]
 

time: 277 us -> 249 us (0.90)
  Pallas kernels: 268 us -> 241 us
    pallas_call x1, Pallas kernels: 268 us -> 241 us  [update(): pl.pallas_call(kernel, out_shape=(squares, squares), in_specs=[smem, hbm,...]
where the time goes in v3:
time: 249 us; the launch traced here: 246 us
  Pallas kernels  241 us (97%)
  local copies, waits for them, and re-layouts  3.74 us (2%)
    pallas_call x1, Pallas kernels, update(): pl.pallas_call(kernel, out_shape=(squares, squares), in_specs=[smem, hbm,...  241 us

profile of v3, /device:TPU:1, one launch (start us, length us, event | category | flops | bytes accessed | tf_op | source)
XLA Modules:
  0.0 245.8 jit_solution(17380747156429083632)
XLA Ops:
  0.6 241.4 %shard_map.77 = (f32[8,128,128]{2,1,0:T(8,128)}, f32[8,128,128]{2,1,0:T(8,128)}) custom-call(s32[8]{0:T(128)} %bitcast.13, bf16[4,8,2,128,128]{4,3,2,1,0:T(8,128)(2,1)} %bitcast.11, bf16[4,2048,128]{2,1,0:T(8,128)(2,1)} %bitcast.12, bf16[8,2048,128]{2,1,0:T(8,128)(2,1)} %bitcast.9, bf16[8,2048,128]{2,1,0:T(8,128)(2,1)} %bitcast.10, bf16[2048,128]{1,0:T(8,128)(2,1)} %refs_5_.1), custom_call_target="tpu_custom_call" | custom-call | flops 12999999488 | bytes 30000000 | tf_op jit(solution)/shard_map/pallas_call | solution.py:606
  242.0 1.9 copy.10
  243.9 1.9 copy.11

commit v4 on v3

--- a/solution.py
+++ b/solution.py
@@ -136,17 +136,20 @@
     def own(self, n):
         return self.part.at[position(n), self.at.core]
 
-    def offer(self, n):
+    def to_sibling(self, n):
         at = self.at
-        copy = remote(
+        return remote(
             self.part.at[position(n), 1 - at.core], self.sibbuf.at[n],
             self.i_send.at[n], self.i_recv.at[n], at.row, at.sib,
         )
+
+    def offer(self, n):
+        copy = self.to_sibling(n)
         copy.start()
         self.inner.append(copy)
 
     def merge(self, n):
-        self.inner[n].wait_recv()
+        arrived(self.sibbuf.at[n], self.i_recv.at[n])
         own = self.own(n)
         own[...] = own[...] + self.sibbuf[n]
 
@@ -204,19 +207,20 @@
         own[...] = own[...] + self.last[...]
         return own
 
-    def run(self, compute, between=None):
+    def run(self, compute):
         for n in range(8):
             compute(n)
             self.offer(n)
             if 1 <= n <= 4:
                 self.act(n - 1)
+        return self.rest()
+
+    def rest(self):
         self.relay(1)
         for n in range(4, 8):
             self.act(n)
         self.finish(1)
         self.relay(0)
-        if between is not None:
-            between()
         self.finish(0)
         return self.total()
 
@@ -302,29 +306,32 @@
     for i in range(8):
         arrived(vbuf.at[:, pl.ds(i * 128, 128)], v_recv.at[i])
 
-    def gram_half(half, write):
+    def gram_pair(pair, half):
         right = vbuf[:, pl.ds(pl.multiple_of(half * 512, 512), 512)]
-        for pair in range(4):
-            value = dot_t(vbuf[:, pl.ds(pair * 256, 256)], right)
-            for p in range(2):
-                write(pair * 2 + p, value[p * 128 : p * 128 + 128])
-
-    def write_out(i, value):
-        part[i, 0, :, :512] = value
-
-    def write_own(i, value):
-        for j in range(4):
-            gown[i, j] = value[:, j * 128 : j * 128 + 128]
-
-    gram_half(1 - core, write_out)
-    g_copy = remote(part.at[:, 0, :, LOW], gsib, g_send, g_recv, row, sib)
-    g_copy.start()
-    gram_half(core, write_own)
-    g_copy.wait_recv()
+        return dot_t(vbuf[:, pl.ds(pair * 256, 256)], right)
+
+    g_copies = []
+    for pair in range(4):
+        value = gram_pair(pair, 1 - core)
+        for p in range(2):
+            part[pair * 2 + p, 0, :, :512] = value[p * 128 : p * 128 + 128]
+        two = pl.ds(pair * 2, 2)
+        copy = remote(
+            part.at[two, 0, :, LOW], gsib.at[two], g_send.at[pair], g_recv.at[pair], row, sib
+        )
+        copy.start()
+        g_copies.append(copy)
+    for pair in range(4):
+        value = gram_pair(pair, core)
+        for p in range(2):
+            for j in range(4):
+                gown[pair * 2 + p, j] = value[p * 128 : p * 128 + 128, j * 128 : j * 128 + 128]
     for j in range(4):
         arrived(sbuf.at[j], s_recv.at[j])
     c_copies = []
     for i in range(8):
+        if i % 2 == 0:
+            g_copies[i // 2].wait_recv()
         for j in range(4):
             total = gown[i, j] + gsib[i, :, j * 128 : j * 128 + 128]
             gown[i, j] = total
@@ -355,7 +362,8 @@
         )
         copy.start()
         c_copies.append(copy)
-    g_copy.wait_send()
+    for copy in g_copies:
+        copy.wait_send()
 
     u_copies = []
 
@@ -410,28 +418,40 @@
         value = sample[c] - dsum[cols_ref[c]]
         sample[c] = value
         gpart[c] = dot_t(value, value, HIGHEST)
-        for h in range(2):
-            copy = Send(
-                gpart.at[c], grbuf.at[me], gr_send.at[c * 2 + h], gr_recv.at[me],
-                row, c * 2 + h, me == c * 2 + h,
-            )
-            copy.start()
-            gram_copies.append(copy)
+        to = c * 2 + c % 2
+        copy = Send(
+            gpart.at[c], grbuf.at[me], gr_send.at[c], gr_recv.at[me], row, to, me == to
+        )
+        copy.start()
+        gram_copies.append(copy)
     second_leg()
-    gram = jnp.zeros((128, 128), F32)
-    for m in range(16):
-        arrived(grbuf.at[m], gr_recv.at[m])
-        gram = gram + grbuf[m]
-    inverse_factor(gram, work, inv)
-
+    factors = core == lax.rem(at.chip, 2)
     l_copies = []
     for n, step in enumerate(ORDER[:7]):
-        copy = remote(
-            inv, lbuf.at[at.chip], l_send.at[n], l_recv.at[at.chip], row, at.inner_at(*step)
-        )
-        copy.start()
-        l_copies.append(copy)
-    lbuf[at.chip] = inv[...]
+        for h in range(2):
+            l_copies.append(
+                remote(
+                    inv, lbuf.at[at.chip], l_send.at[n * 2 + h], l_recv.at[at.chip],
+                    row, at.chip_at(*step) * 2 + h,
+                )
+            )
+    l_copies.append(remote(inv, lbuf.at[at.chip], l_send.at[14], l_recv.at[at.chip], row, sib))
+
+    @pl.when(factors)
+    def _():
+        gram = jnp.zeros((128, 128), F32)
+        for m in range(16):
+            arrived(grbuf.at[m], gr_recv.at[m])
+            gram = gram + grbuf[m]
+        inverse_factor(gram, work, inv)
+        for copy in l_copies:
+            copy.start()
+        lbuf[at.chip] = inv[...]
+
+    @pl.when(jnp.logical_not(factors))
+    def _():
+        arrived(lbuf.at[at.chip], l_recv.at[at.chip])
+
     third_leg()
     for step in ORDER[:7]:
         source = at.chip_at(*step)
@@ -539,15 +559,31 @@
                     y * 128 : y * 128 + 128
                 ]
 
-    terms(1, half_z, cols_ref)
-    terms(0, half_z, cols_ref)
-    arrived(their_cols, cols_sem.at[1])
-    for kk in range(4):
-        arrived(ib.at[1 - half_z, pl.ds(kk * 128, 128), :], i_recv.at[kk])
-
-    def r_block(n):
-        if n % 4 == 0:
-            terms(1 - n // 4, 1 - half_z, their_cols)
+    mine = core == half_z
+    others = core != half_z
+
+    def projection():
+        return Reduction(
+            at, part, sibbuf, vbuf, r_hops, r_last, (ri_send, ri_recv, r_send, r_recv)
+        )
+
+    offers = [projection().to_sibling(n) for n in range(8)]
+    for s in range(2):
+        terms(1 - s, half_z, cols_ref)
+
+        @pl.when(others)
+        def _():
+            for n in range(4):
+                offers[s * 4 + n].start()
+
+    @pl.when(mine)
+    def _():
+        sums = projection()
+        for n in range(4):
+            sums.act(n)
+        sums.rest()
+        for copy in sums.copies:
+            copy.wait_send()
 
     def p_basis():
         for t in range(2):
@@ -563,34 +599,52 @@
 
     load_tiles.wait()
     load_q.wait()
-    projection = Reduction(
-        at, part, sibbuf, vbuf, r_hops, r_last, (ri_send, ri_recv, r_send, r_recv)
-    )
-    total = projection.run(r_block, p_basis)
+    p_basis()
+    arrived(their_cols, cols_sem.at[1])
+    for kk in range(4):
+        arrived(ib.at[1 - half_z, pl.ds(kk * 128, 128), :], i_recv.at[kk])
+    for s in range(2):
+        terms(1 - s, 1 - half_z, their_cols)
+
+        @pl.when(mine)
+        def _():
+            for n in range(4):
+                offers[s * 4 + n].start()
 
     def write_right(source):
         for c in range(8):
             right_ref[c] = (sample[c] - source[:, c * 128 : c * 128 + 128]) * (1.0 / scale)
 
-    swap = remote(total, swapped, t_send, t_recv, partner, sib)
-
-    @pl.when(core == half_z)
+    @pl.when(mine)
     def _():
-        write_right(total)
-
-    @pl.when(core != half_z)
+        write_right(projection().own(7))
+
+    @pl.when(others)
     def _():
+        sums = projection()
+        for n in range(4):
+            sums.act(n)
+        swap = remote(sums.rest(), swapped, t_send, t_recv, partner, sib)
         swap.start()
+        for copy in sums.copies:
+            copy.wait_send()
         swap.wait_recv()
         write_right(swapped)
         swap.wait_send()
 
+    for copy in offers:
+        copy.wait_send()
     cols_copy.wait_send()
-    for copy in v_copies + s_copies + c_copies + u_copies + gram_copies + l_copies:
+
+    @pl.when(factors)
+    def _():
+        for copy in l_copies:
+            copy.wait_send()
+
+    for copy in v_copies + s_copies + c_copies + u_copies + gram_copies:
         copy.wait_send()
     for copy in b_copies + f_copies + i_copies:
         copy.wait_send()
-    projection.wait_sends()
 
 
 def update(u, v, p, q, sketch, cols, scale):
@@ -638,10 +692,10 @@
             pltpu.VMEM((128, 1024), BF16),
             pltpu.VMEM((2048, 1024), BF16),
             pltpu.VMEM((2, 512, 1024), BF16),
-            dma((5,)), dma((8,)), dma((8,)), dma((4,)), dma((4,)), dma, dma,
+            dma((5,)), dma((8,)), dma((8,)), dma((4,)), dma((4,)), dma((4,)), dma((4,)),
             dma((8,)), dma((8,)), dma((8,)), dma((8,)),
             dma((9,)), dma((9,)), dma((8,)), dma((8,)), dma((13,)), dma((13,)),
-            dma((16,)), dma((16,)), dma((7,)), dma((8,)),
+            dma((8,)), dma((16,)), dma((15,)), dma((8,)),
             dma((9,)), dma((5,)), dma((4,)), dma((10,)), dma((10,)),
             dma((8,)), dma((8,)), dma((13,)), dma((13,)),
             pltpu.VMEM((4, 8, 2, 128, 128), BF16),

time: 249 us -> 243 us (0.976)
  Pallas kernels: 241 us -> 236 us
    pallas_call x1, Pallas kernels: 241 us -> 236 us  [update(): pl.pallas_call(kernel, out_shape=(squares, squares), in_specs=[smem, hbm,...]
where the time goes in v4:
time: 243 us; the launch traced here: 241 us
  Pallas kernels  236 us (97%)
  local copies, waits for them, and re-layouts  3.74 us (2%)
    pallas_call x1, Pallas kernels, update(): pl.pallas_call(kernel, out_shape=(squares, squares), in_specs=[smem, hbm,...  236 us

profile of v4, /device:TPU:1, one launch (start us, length us, event | category | flops | bytes accessed | tf_op | source)
XLA Modules:
  0.0 240.6 jit_solution(9966406708176189038)
XLA Ops:
  0.6 236.2 %shard_map.77 = (f32[8,128,128]{2,1,0:T(8,128)}, f32[8,128,128]{2,1,0:T(8,128)}) custom-call(s32[8]{0:T(128)} %bitcast.13, bf16[4,8,2,128,128]{4,3,2,1,0:T(8,128)(2,1)} %bitcast.11, bf16[4,2048,128]{2,1,0:T(8,128)(2,1)} %bitcast.12, bf16[8,2048,128]{2,1,0:T(8,128)(2,1)} %bitcast.9, bf16[8,2048,128]{2,1,0:T(8,128)(2,1)} %bitcast.10, bf16[2048,128]{1,0:T(8,128)(2,1)} %refs_5_.1), custom_call_target="tpu_custom_call" | custom-call | flops 12999999488 | bytes 30000000 | tf_op jit(solution)/shard_map/pallas_call | solution.py:660
  236.9 1.9 copy.10
  238.8 1.9 copy.11

commit v5 on v4

--- a/solution.py
+++ b/solution.py
@@ -102,7 +102,7 @@
 
 def inverse_factor(gram, work, inv):
     order = gram.shape[0]
-    strip = 16
+    strip, group = 16, 4
     row_id = lax.broadcasted_iota(jnp.int32, (order, order), 0)
     col_id = lax.broadcasted_iota(jnp.int32, (order, order), 1)
     diagonal = row_id == col_id
@@ -110,14 +110,39 @@
     work[...] = gram + jnp.where(diagonal, ridge, 0.0)
     inv[...] = jnp.where(diagonal, 1.0, 0.0)
     within = lax.broadcasted_iota(jnp.int32, (strip, order), 0)
+    full = (strip, order)
     for lo in range(0, order, strip):
         a, m = work[lo : lo + strip, :], inv[lo : lo + strip, :]
-        for j in range(strip):
-            scale = lax.rsqrt(a[j : j + 1, lo + j : lo + j + 1])
-            a_row, m_row = a[j : j + 1, :] * scale, m[j : j + 1, :] * scale
-            factor = jnp.where(within > j, a[:, lo + j : lo + j + 1] * scale, 0.0)
-            a = jnp.where(within == j, a_row, a - factor * a_row)
-            m = jnp.where(within == j, m_row, m - factor * m_row)
+        for first in range(0, strip, group):
+            cols, rows, m_rows = [], [], []
+            for k in range(group):
+                at_col, at_row = lo + first + k, first + k
+                cols.append(jnp.broadcast_to(a[:, at_col : at_col + 1], full))
+                rows.append(jnp.broadcast_to(a[at_row : at_row + 1, :], full))
+                m_rows.append(jnp.broadcast_to(m[at_row : at_row + 1, :], full))
+            small = {}
+            for k in range(group):
+                for i in range(k, group):
+                    at_row = first + i
+                    value = jnp.broadcast_to(cols[k][at_row : at_row + 1, :], full)
+                    for p in range(k):
+                        value = value - small[i, p] * small[k, p]
+                    small[i, k] = lax.rsqrt(value) if i == k else value * small[k, k]
+            for k in range(group):
+                for p in range(k):
+                    cols[k] = cols[k] - small[k, p] * cols[p]
+                    rows[k] = rows[k] - small[k, p] * rows[p]
+                    m_rows[k] = m_rows[k] - small[k, p] * m_rows[p]
+                cols[k] = cols[k] * small[k, k]
+                rows[k] = rows[k] * small[k, k]
+                m_rows[k] = m_rows[k] * small[k, k]
+            below = within >= first + group
+            for k in range(group):
+                factor = jnp.where(below, cols[k], 0.0)
+                a, m = a - factor * rows[k], m - factor * m_rows[k]
+            for k in range(group):
+                here = within == first + k
+                a, m = jnp.where(here, rows[k], a), jnp.where(here, m_rows[k], m)
         inv[lo : lo + strip, :] = m
         rest = lo + strip
         if rest < order:
@@ -266,7 +291,7 @@
 
     v_copies = []
     for n in range(8):
-        kk, hh = lax.rem(slot + n // 2, 4), lax.rem(n + core, 2)
+        kk, hh = lax.rem(slot + n % 4, 4), lax.rem(n // 4 + core, 2)
         to = core * 4 + kk
         copy = Send(
             v_ref.at[kk, pl.ds(pl.multiple_of(hh * 1024, 1024), 1024), :],
@@ -354,14 +379,6 @@
             arrived(
                 coupled.at[pl.ds(kk * 128, 128), pl.ds(hh * 512, 512)], c_recv.at[kk * 2 + hh]
             )
-    for i in range(8):
-        copy = Send(
-            gown.at[i], coupling.at[slot, pl.ds(core * 4, 4)],
-            k_send.at[i], k_recv.at[slot * 2 + core], i, base + owner_core,
-            jnp.logical_and(row == i, core == owner_core),
-        )
-        copy.start()
-        c_copies.append(copy)
     for copy in g_copies:
         copy.wait_send()
 
@@ -385,6 +402,15 @@
     u_copies.append(copy)
     pass_panel(row, None, 1, 0)
     pass_panel(row, None, 3, 0)
+
+    for i in range(8):
+        copy = Send(
+            gown.at[i], coupling.at[slot, pl.ds(core * 4, 4)],
+            k_send.at[i], k_recv.at[slot * 2 + core], i, base + owner_core,
+            jnp.logical_and(row == i, core == owner_core),
+        )
+        copy.start()
+        c_copies.append(copy)
 
     def d_block(n):
         chip = at.chip_at(*ORDER[n])
@@ -452,7 +478,6 @@
     def _():
         arrived(lbuf.at[at.chip], l_recv.at[at.chip])
 
-    third_leg()
     for step in ORDER[:7]:
         source = at.chip_at(*step)
         arrived(lbuf.at[source], l_recv.at[source])
@@ -508,6 +533,7 @@
                 value = dot_t(u_own[kk, chip].reshape(256, 128), basis[rows, h * 512 : h * 512 + 512])
                 gsib[kk * 2 + h] = value if first else gsib[kk * 2 + h] + value
 
+    third_leg()
     basis_term(0, 0, 0, True)
     basis_term(1, 1, 0)
     basis_term(2, 0, 3)

time: 243 us -> 234 us (0.963)
  Pallas kernels: 236 us -> 228 us
    pallas_call x1, Pallas kernels: 236 us -> 228 us  [update(): pl.pallas_call(kernel, out_shape=(squares, squares), in_specs=[smem, hbm,...]
where the time goes in v5:
time: 234 us; the launch traced here: 232 us
  Pallas kernels  228 us (97%)
  local copies, waits for them, and re-layouts  3.74 us (2%)
    pallas_call x1, Pallas kernels, update(): pl.pallas_call(kernel, out_shape=(squares, squares), in_specs=[smem, hbm,...  228 us

profile of v5, /device:TPU:1, one launch (start us, length us, event | category | flops | bytes accessed | tf_op | source)
XLA Modules:
  0.0 232.1 jit_solution(422855827750102237)
XLA Ops:
  0.6 227.7 %shard_map.77 = (f32[8,128,128]{2,1,0:T(8,128)}, f32[8,128,128]{2,1,0:T(8,128)}) custom-call(s32[8]{0:T(128)} %bitcast.13, bf16[4,8,2,128,128]{4,3,2,1,0:T(8,128)(2,1)} %bitcast.11, bf16[4,2048,128]{2,1,0:T(8,128)(2,1)} %bitcast.12, bf16[8,2048,128]{2,1,0:T(8,128)(2,1)} %bitcast.9, bf16[8,2048,128]{2,1,0:T(8,128)(2,1)} %bitcast.10, bf16[2048,128]{1,0:T(8,128)(2,1)} %refs_5_.1), custom_call_target="tpu_custom_call" | custom-call | flops 12999999488 | bytes 30000000 | tf_op jit(solution)/shard_map/pallas_call | solution.py:686
  228.3 1.9 copy.10
  230.2 1.9 copy.11

commit v6 on v5

--- a/solution.py
+++ b/solution.py
@@ -403,15 +403,6 @@
     pass_panel(row, None, 1, 0)
     pass_panel(row, None, 3, 0)
 
-    for i in range(8):
-        copy = Send(
-            gown.at[i], coupling.at[slot, pl.ds(core * 4, 4)],
-            k_send.at[i], k_recv.at[slot * 2 + core], i, base + owner_core,
-            jnp.logical_and(row == i, core == owner_core),
-        )
-        copy.start()
-        c_copies.append(copy)
-
     def d_block(n):
         chip = at.chip_at(*ORDER[n])
         left = jnp.concatenate([u_own[kk, chip].reshape(256, 128) for kk in range(4)], axis=1)
@@ -451,6 +442,15 @@
         copy.start()
         gram_copies.append(copy)
     second_leg()
+    for i in range(8):
+        copy = Send(
+            gown.at[i], coupling.at[slot, pl.ds(core * 4, 4)],
+            k_send.at[i], k_recv.at[slot * 2 + core], i, base + owner_core,
+            jnp.logical_and(row == i, core == owner_core),
+        )
+        copy.start()
+        c_copies.append(copy)
+
     factors = core == lax.rem(at.chip, 2)
     l_copies = []
     for n, step in enumerate(ORDER[:7]):
@@ -533,13 +533,13 @@
                 value = dot_t(u_own[kk, chip].reshape(256, 128), basis[rows, h * 512 : h * 512 + 512])
                 gsib[kk * 2 + h] = value if first else gsib[kk * 2 + h] + value
 
-    third_leg()
     basis_term(0, 0, 0, True)
     basis_term(1, 1, 0)
     basis_term(2, 0, 3)
     basis_term(3, 0, 1)
     basis_term(4, 1, 3)
     basis_term(5, 1, 1)
+    third_leg()
     for s in range(2):
         m = at.inner_at(s, 2)
         for way in range(2):

time: 234 us -> 233 us (level)
  Pallas kernels: 228 us -> 224 us
    pallas_call x1, Pallas kernels: 228 us -> 224 us  [update(): pl.pallas_call(kernel, out_shape=(squares, squares), in_specs=[smem, hbm,...]
where the time goes in v6:
time: 233 us; the launch traced here: 229 us
  Pallas kernels  224 us (96%)
  local copies, waits for them, and re-layouts  3.74 us (2%)
    pallas_call x1, Pallas kernels, update(): pl.pallas_call(kernel, out_shape=(squares, squares), in_specs=[smem, hbm,...  224 us

profile of v6, /device:TPU:1, one launch (start us, length us, event | category | flops | bytes accessed | tf_op | source)
XLA Modules:
  0.0 228.9 jit_solution(5496930855800608241)
XLA Ops:
  0.6 224.5 %shard_map.77 = (f32[8,128,128]{2,1,0:T(8,128)}, f32[8,128,128]{2,1,0:T(8,128)}) custom-call(s32[8]{0:T(128)} %bitcast.13, bf16[4,8,2,128,128]{4,3,2,1,0:T(8,128)(2,1)} %bitcast.11, bf16[4,2048,128]{2,1,0:T(8,128)(2,1)} %bitcast.12, bf16[8,2048,128]{2,1,0:T(8,128)(2,1)} %bitcast.9, bf16[8,2048,128]{2,1,0:T(8,128)(2,1)} %bitcast.10, bf16[2048,128]{1,0:T(8,128)(2,1)} %refs_5_.1), custom_call_target="tpu_custom_call" | custom-call | flops 12999999488 | bytes 30000000 | tf_op jit(solution)/shard_map/pallas_call | solution.py:686
  225.1 1.9 copy.10
  227.0 1.9 copy.11

commit v7 on v6

--- a/solution.py
+++ b/solution.py
@@ -442,14 +442,6 @@
         copy.start()
         gram_copies.append(copy)
     second_leg()
-    for i in range(8):
-        copy = Send(
-            gown.at[i], coupling.at[slot, pl.ds(core * 4, 4)],
-            k_send.at[i], k_recv.at[slot * 2 + core], i, base + owner_core,
-            jnp.logical_and(row == i, core == owner_core),
-        )
-        copy.start()
-        c_copies.append(copy)
 
     factors = core == lax.rem(at.chip, 2)
     l_copies = []
@@ -478,6 +470,14 @@
     def _():
         arrived(lbuf.at[at.chip], l_recv.at[at.chip])
 
+    for i in range(8):
+        copy = Send(
+            gown.at[i], coupling.at[slot, pl.ds(core * 4, 4)],
+            k_send.at[i], k_recv.at[slot * 2 + core], i, base + owner_core,
+            jnp.logical_and(row == i, core == owner_core),
+        )
+        copy.start()
+        c_copies.append(copy)
     for step in ORDER[:7]:
         source = at.chip_at(*step)
         arrived(lbuf.at[source], l_recv.at[source])

time: 233 us -> 233 us (level)
  no operation moved by 1% of the time
where the time goes in v7:
time: 233 us; the launch traced here: 229 us
  Pallas kernels  224 us (96%)
  local copies, waits for them, and re-layouts  3.74 us (2%)
    pallas_call x1, Pallas kernels, update(): pl.pallas_call(kernel, out_shape=(squares, squares), in_specs=[smem, hbm,...  224 us

profile of v7, /device:TPU:1, one launch (start us, length us, event | category | flops | bytes accessed | tf_op | source)
XLA Modules:
  0.0 228.9 jit_solution(4356769529990570609)
XLA Ops:
  0.6 224.5 %shard_map.77 = (f32[8,128,128]{2,1,0:T(8,128)}, f32[8,128,128]{2,1,0:T(8,128)}) custom-call(s32[8]{0:T(128)} %bitcast.13, bf16[4,8,2,128,128]{4,3,2,1,0:T(8,128)(2,1)} %bitcast.11, bf16[4,2048,128]{2,1,0:T(8,128)(2,1)} %bitcast.12, bf16[8,2048,128]{2,1,0:T(8,128)(2,1)} %bitcast.9, bf16[8,2048,128]{2,1,0:T(8,128)(2,1)} %bitcast.10, bf16[2048,128]{1,0:T(8,128)(2,1)} %refs_5_.1), custom_call_target="tpu_custom_call" | custom-call | flops 12999999488 | bytes 30000000 | tf_op jit(solution)/shard_map/pallas_call | solution.py:686
  225.1 1.9 copy.10
  227.0 1.9 copy.11

commit v8 on v7

--- a/solution.py
+++ b/solution.py
@@ -537,9 +537,9 @@
     basis_term(1, 1, 0)
     basis_term(2, 0, 3)
     basis_term(3, 0, 1)
+    third_leg()
     basis_term(4, 1, 3)
     basis_term(5, 1, 1)
-    third_leg()
     for s in range(2):
         m = at.inner_at(s, 2)
         for way in range(2):

time: 233 us -> 233 us (level)
  no operation moved by 1% of the time
where the time goes in v8:
time: 233 us; the launch traced here: 229 us
  Pallas kernels  224 us (96%)
  local copies, waits for them, and re-layouts  3.74 us (2%)
    pallas_call x1, Pallas kernels, update(): pl.pallas_call(kernel, out_shape=(squares, squares), in_specs=[smem, hbm,...  224 us

profile of v8, /device:TPU:1, one launch (start us, length us, event | category | flops | bytes accessed | tf_op | source)
XLA Modules:
  0.0 228.9 jit_solution(15092469100527885169)
XLA Ops:
  0.6 224.5 %shard_map.77 = (f32[8,128,128]{2,1,0:T(8,128)}, f32[8,128,128]{2,1,0:T(8,128)}) custom-call(s32[8]{0:T(128)} %bitcast.13, bf16[4,8,2,128,128]{4,3,2,1,0:T(8,128)(2,1)} %bitcast.11, bf16[4,2048,128]{2,1,0:T(8,128)(2,1)} %bitcast.12, bf16[8,2048,128]{2,1,0:T(8,128)(2,1)} %bitcast.9, bf16[8,2048,128]{2,1,0:T(8,128)(2,1)} %bitcast.10, bf16[2048,128]{1,0:T(8,128)(2,1)} %refs_5_.1), custom_call_target="tpu_custom_call" | custom-call | flops 12999999488 | bytes 30000000 | tf_op jit(solution)/shard_map/pallas_call | solution.py:686
  225.1 1.9 copy.10
  227.0 1.9 copy.11
